TPU v7x, 128 devices: a whole 4x4x4 slice. The times are simulated.
128 devices in a mesh: gx: 16 (over y, x), gy: 8 (over z, core).
Axes of the slice: x: 4, y: 4, z: 4, core: 2. Of those that a mesh axis runs over, the one named last changes fastest.
Arguments:
- waveforms: bfloat16 [256, 3, 1536], P(('gx', 'gy')), may hold values from -100 to 100
- templates: bfloat16 [4096, 8, 1536], P(('gx', 'gy')), may hold values from -100 to 100
- tpl_stations: int32 [4096, 8], P(('gx', 'gy')), may hold values from 0 to 255, all different within a row; in each aligned block of 32 rows (0 to 31, 32 to 63, ...) at most 2 rows name the same one
- det_station: int32 [8192], P(('gx', 'gy')), may hold values from 0 to 1
- det_time: int32 [8192], P(('gx', 'gy')), may hold values from 64 to 1216
- partner: int32 [8192, 4], P(('gx', 'gy')), may hold values from 0 to 63
Outputs:
- stack: float32 [4096, 1024], P(('gx', 'gy'))
- diffcc: float32 [8192, 4, 128], P(('gx', 'gy'))
Inputs may be any that keep to these rules, and one draw needn't show every extreme that they name: `tpl_stations`: each row names 8 different stations; among the templates of one station group no station is named more than 2 times.
All inputs are finite; a program needn't handle non-finite values.
Results may differ from a plain program's by a relative error of at most 0.0007.
Values may be sent and summed in bfloat16 or wider, within the bound.
A program may use at most 128 MiB of HBM per device.

v0:
```python
import jax
import jax.numpy as jnp
from jax import lax
from jax.sharding import PartitionSpec as P

W = 256
DTLAG = 128


def from_behind(value, axis, steps):
    count = lax.axis_size(axis)
    leading, last = (max(0, -steps), min(count, count - steps))
    return lax.ppermute(value, axis, [(source, source + steps) for source in range(leading, last)])


def lagged_rows(series, rows, lags):
    length = series.shape[-1]
    lead = series.shape[:-1]
    tiled = jnp.tile(series, (1,) * len(lead) + (rows + 1,))
    tiled = tiled[..., : rows * (length + 1)].reshape(lead + (rows, length + 1))
    return tiled[..., :lags]


def on_device(waveforms, templates, tpl_stations, det_station, det_time, partner):
    sta_dev = waveforms.shape[0]
    samples = waveforms.shape[2]
    tpl_dev, k_slots, row_len = templates.shape
    tlen = row_len // 3
    nlag = samples - tlen
    ngx = lax.axis_size("gx")
    ngy = lax.axis_size("gy")
    groups = ngx * ngy
    stations = sta_dev * groups
    cap = max(2, (2 * tpl_dev * k_slots + stations - 1) // stations)
    flat_station = tpl_stations.reshape(-1)
    count = flat_station.shape[0]
    order = jnp.arange(count, dtype=jnp.int32)
    same = (flat_station[:, None] == flat_station[None, :]) & (order[None, :] < order[:, None])
    rank = jnp.sum(same.astype(jnp.int32), axis=1)
    owner = flat_station // sta_dev
    within = flat_station % sta_dev
    slot = (within * groups + owner) * cap + rank
    outbox = jnp.zeros((sta_dev * groups * cap, row_len), jnp.bfloat16)
    outbox = outbox.at[slot].set(templates.reshape(count, row_len))
    inbox = lax.all_to_all(
        outbox.reshape(sta_dev, groups, cap, row_len),
        ("gx", "gy"),
        split_axis=1,
        concat_axis=1,
        tiled=True,
    )
    inbox = inbox.reshape(sta_dev, groups * cap, row_len)

    def correlate(pair):
        station_data, tiles = pair
        lagged = lagged_rows(station_data, tlen, nlag).reshape(3 * tlen, nlag)
        raw = jnp.dot(tiles, lagged, preferred_element_type=jnp.float32)
        tile_mean = jnp.einsum("mr,mr->m", tiles, tiles, preferred_element_type=jnp.float32) / (
            3 * tlen
        )
        values = station_data.astype(jnp.float32)
        energy = jnp.sum(values * values, axis=0)
        window_sum = lax.reduce_window(energy, jnp.float32(0.0), lax.add, (tlen,), (1,), "VALID")
        win_mean = window_sum[:nlag] / (3 * tlen)
        return (
            raw
            * lax.rsqrt(3 * tlen * (tile_mean + 1e-06))[:, None]
            * lax.rsqrt(win_mean + 1e-06)[None, :]
        )

    traces = lax.map(correlate, (waveforms, inbox))
    returned = lax.all_to_all(
        traces.reshape(sta_dev, groups, cap, nlag),
        ("gx", "gy"),
        split_axis=1,
        concat_axis=1,
        tiled=True,
    )
    picked = returned.reshape(sta_dev * groups * cap, nlag)[slot]
    stack = jnp.sum(picked.reshape(tpl_dev, k_slots, nlag), axis=1) / jnp.sqrt(jnp.float32(k_slots))
    half = DTLAG // 2
    wide_len = W + DTLAG
    det_dev = det_station.shape[0]

    def cut(sta, start, size):
        return lax.dynamic_slice(waveforms, (sta, jnp.int32(0), start), (1, 3, size))[0]

    local = jax.vmap(lambda s, t: cut(s, t, W))(det_station, det_time)
    wide = jax.vmap(lambda s, t: cut(s, t - half, wide_len))(det_station, det_time)
    across = [from_behind(wide, "gx", step) for step in (-1, 1)]
    along = [from_behind(wide, "gy", step) for step in (-1, 1)]
    received = jnp.stack([across[0], across[1], along[0], along[1]])
    chosen = jax.vmap(lambda rows, picks: rows[picks])(received, partner.T)
    pieces = chosen.reshape(4 * det_dev, 3, wide_len)
    locals_all = jnp.broadcast_to(local[None], (4, det_dev, 3, W)).reshape(4 * det_dev, 3, W)
    blocks = 4 * det_dev // 16

    def window_block(pair):
        piece, mine = pair
        lagged = lagged_rows(piece, W, DTLAG)
        raw = jnp.einsum("bct,bctl->bl", mine, lagged, preferred_element_type=jnp.float32)
        mine_mean = jnp.einsum("bct,bct->b", mine, mine, preferred_element_type=jnp.float32) / (
            3 * W
        )
        centre = piece[:, :, half : half + W]
        piece_mean = jnp.einsum(
            "bct,bct->b", centre, centre, preferred_element_type=jnp.float32
        ) / (3 * W)
        return (
            raw
            * lax.rsqrt(3 * W * (mine_mean + 1e-06))[:, None]
            * lax.rsqrt(piece_mean + 1e-06)[:, None]
        )

    result = lax.map(
        window_block,
        (pieces.reshape(blocks, 16, 3, wide_len), locals_all.reshape(blocks, 16, 3, W)),
    )
    diffcc = jnp.transpose(result.reshape(4, det_dev, DTLAG), (1, 0, 2))
    return (stack, diffcc)


def solution(mesh):
    return jax.shard_map(
        on_device,
        mesh=mesh,
        in_specs=(
            P(("gx", "gy"), None, None),
            P(("gx", "gy"), None, None),
            P(("gx", "gy"), None),
            P(("gx", "gy")),
            P(("gx", "gy")),
            P(("gx", "gy"), None),
        ),
        out_specs=(P(("gx", "gy"), None), P(("gx", "gy"), None, None)),
        check_vma=False,
    )
```

profile of v0, /device:TPU:1, one launch (start us, length us, event | category | flops | bytes accessed | tf_op | source)
XLA Modules:
  0.0 1257.2 jit_solution(16685991721860048661)
XLA Ops:
  9.4 11.8 all-to-all-start
  21.9 19.2 %gather_fusion.2 = bf16[64,3,384]{1,0,2:T(8,128)(2,1)} fusion(bf16[2,3,1536]{1,0,2:T(2,128)(2,1)S(1)} %copy.67, s32[64]{0:T(128)S(1)} %get-tuple-element.112), kind=kCustom, calls=%fused_computation.2 | custom fusion | bytes 295680 | tf_op jit(solution)/shard_map/vmap()/gather | solution.py:86
  41.1 8.7 copy.70
  61.4 13.1 %gather_fusion.1 = bf16[64,3,256]{1,0,2:T(8,128)(2,1)} fusion(bf16[2,3,1536]{1,0,2:T(2,128)(2,1)S(1)} %copy.67, s32[64]{0:T(128)S(1)} %get-tuple-element.113), kind=kCustom, calls=%fused_computation.1 | custom fusion | bytes 197376 | tf_op jit(solution)/shard_map/vmap()/gather | solution.py:86
  89.4 271.5 %while.20 = (s32[]{:T(128)}, f32[2,256,1024]{2,0,1:T(2,128)}, bf16[2,256,1536]{2,1,0:T(8,128)(2,1)S(1)}, bf16[2,3,1536]{2,1,0:T(4,128)(2,1)S(1)}, s32[]{:T(128)}, /*index=5*/f32[]{:T(128)}, s32[]{:T(128)}) while((s32[]{:T(128)}, f32[2,256,1024]{2,0,1:T(2,128)}, bf16[2,256,1536]{2,1,0:T(8,128)(2,1)S(1)}, bf16[2,3,1536]{2,1,0:T(4,128)(2,1)S(1)}, ...), condition=%wide.region_5.6_spmd, body=%wide.region_2.5_spmd.sunk | while | flops 807548928 | bytes 58986652 | solution.py:71
  101.8 9.1 reshape.278
  110.9 11.7 reshape.279
  126.7 71.3 %reduce-window.6 = f32[1025,1]{1,0:T(8,128)S(1)} reduce-window(f32[1536,1]{1,0:T(8,128)S(1)} %reshape.280, f32[]{:T(128)} %constant.49.clone.2..sunk), window={size=512x1}, to_apply=%region_4.4 | reduce-window | flops 523775 | bytes 10248 | tf_op jit(solution)/shard_map/reduce-window
  202.4 18.7 %dynamic_update_slice.11 = f32[2,256,1024]{2,0,1:T(2,128)} dynamic-update-slice(f32[2,256,1024]{2,0,1:T(2,128)} %get-tuple-element.180, f32[1,256,1024]{2,0,1:T(1,128)S(1)} %copy.104, s32[]{:T(128)} %get-tuple-element.179, s32[]{:T(128)} %constant.82.clone.1..sunk, s32[]{:T(128)} %constant.82.clone.1..sunk) | dynamic-update-slice | bytes 2097156 | tf_op jit(solution)/shard_map/while/body/jit(dynamic_update_index_in_dim)/dynamic_update_slice | solution.py:71
  233.3 9.1 reshape.278
  242.4 12.0 reshape.279
  258.5 71.3 %reduce-window.6 = f32[1025,1]{1,0:T(8,128)S(1)} reduce-window(f32[1536,1]{1,0:T(8,128)S(1)} %reshape.280, f32[]{:T(128)} %constant.49.clone.2..sunk), window={size=512x1}, to_apply=%region_4.4 | reduce-window | flops 523775 | bytes 10248 | tf_op jit(solution)/shard_map/reduce-window
  334.2 18.7 %dynamic_update_slice.11 = f32[2,256,1024]{2,0,1:T(2,128)} dynamic-update-slice(f32[2,256,1024]{2,0,1:T(2,128)} %get-tuple-element.180, f32[1,256,1024]{2,0,1:T(1,128)S(1)} %copy.104, s32[]{:T(128)} %get-tuple-element.179, s32[]{:T(128)} %constant.82.clone.1..sunk, s32[]{:T(128)} %constant.82.clone.1..sunk) | dynamic-update-slice | bytes 2097156 | tf_op jit(solution)/shard_map/while/body/jit(dynamic_update_index_in_dim)/dynamic_update_slice | solution.py:71
  365.0 11.0 all-to-all-start.1
  376.2 870.7 %while.21 = (s32[]{:T(128)}, f32[16,16,128]{2,1,0:T(8,128)S(1)}, bf16[16,16,3,256]{3,2,1,0:T(4,128)(2,1)S(1)}, bf16[16,16,3,384]{3,1,2,0:T(8,128)(2,1)}, s32[]{:T(128)}) while((s32[]{:T(128)}, f32[16,16,128]{2,1,0:T(8,128)S(1)}, bf16[16,16,3,256]{3,2,1,0:T(4,128)(2,1)S(1)}, bf16[16,16,3,384]{3,1,2,0:T(8,128)(2,1)}, s32[]{:T(128)}) %tuple.62), condition=%wide.region_8.9_spmd, body=%wide.region_7.8_spmd.sunk | while | flops 3223602 | bytes 69674432 | solution.py:115
  381.9 10.6 tile.28
  400.6 27.5 %reshape.281 = bf16[16,3,256,385]{3,2,0,1:T(8,128)(2,1)} reshape(bf16[16,3,98560]{2,0,1:T(8,128)(2,1)} %slice.57) | data formatting | bytes 18923520 | tf_op jit(solution)/shard_map/while/body/eval_jaxpr/reshape | solution.py:20
  436.4 10.6 tile.28
  455.0 27.5 %reshape.281 = bf16[16,3,256,385]{3,2,0,1:T(8,128)(2,1)} reshape(bf16[16,3,98560]{2,0,1:T(8,128)(2,1)} %slice.57) | data formatting | bytes 18923520 | tf_op jit(solution)/shard_map/while/body/eval_jaxpr/reshape | solution.py:20
  490.8 10.6 tile.28
  509.4 27.5 %reshape.281 = bf16[16,3,256,385]{3,2,0,1:T(8,128)(2,1)} reshape(bf16[16,3,98560]{2,0,1:T(8,128)(2,1)} %slice.57) | data formatting | bytes 18923520 | tf_op jit(solution)/shard_map/while/body/eval_jaxpr/reshape | solution.py:20
  545.2 10.6 tile.28
  563.8 27.5 %reshape.281 = bf16[16,3,256,385]{3,2,0,1:T(8,128)(2,1)} reshape(bf16[16,3,98560]{2,0,1:T(8,128)(2,1)} %slice.57) | data formatting | bytes 18923520 | tf_op jit(solution)/shard_map/while/body/eval_jaxpr/reshape | solution.py:20
  599.6 10.6 tile.28
  618.3 27.5 %reshape.281 = bf16[16,3,256,385]{3,2,0,1:T(8,128)(2,1)} reshape(bf16[16,3,98560]{2,0,1:T(8,128)(2,1)} %slice.57) | data formatting | bytes 18923520 | tf_op jit(solution)/shard_map/while/body/eval_jaxpr/reshape | solution.py:20
  654.0 10.6 tile.28
  672.7 27.5 %reshape.281 = bf16[16,3,256,385]{3,2,0,1:T(8,128)(2,1)} reshape(bf16[16,3,98560]{2,0,1:T(8,128)(2,1)} %slice.57) | data formatting | bytes 18923520 | tf_op jit(solution)/shard_map/while/body/eval_jaxpr/reshape | solution.py:20
  708.5 10.6 tile.28
  727.1 27.5 %reshape.281 = bf16[16,3,256,385]{3,2,0,1:T(8,128)(2,1)} reshape(bf16[16,3,98560]{2,0,1:T(8,128)(2,1)} %slice.57) | data formatting | bytes 18923520 | tf_op jit(solution)/shard_map/while/body/eval_jaxpr/reshape | solution.py:20
  762.9 10.6 tile.28
  781.5 27.5 %reshape.281 = bf16[16,3,256,385]{3,2,0,1:T(8,128)(2,1)} reshape(bf16[16,3,98560]{2,0,1:T(8,128)(2,1)} %slice.57) | data formatting | bytes 18923520 | tf_op jit(solution)/shard_map/while/body/eval_jaxpr/reshape | solution.py:20
  817.3 10.6 tile.28
  835.9 27.5 %reshape.281 = bf16[16,3,256,385]{3,2,0,1:T(8,128)(2,1)} reshape(bf16[16,3,98560]{2,0,1:T(8,128)(2,1)} %slice.57) | data formatting | bytes 18923520 | tf_op jit(solution)/shard_map/while/body/eval_jaxpr/reshape | solution.py:20
  871.7 10.6 tile.28
  890.4 27.5 %reshape.281 = bf16[16,3,256,385]{3,2,0,1:T(8,128)(2,1)} reshape(bf16[16,3,98560]{2,0,1:T(8,128)(2,1)} %slice.57) | data formatting | bytes 18923520 | tf_op jit(solution)/shard_map/while/body/eval_jaxpr/reshape | solution.py:20
  926.2 10.6 tile.28
  936.8 8.0 slice.57
  944.8 27.5 %reshape.281 = bf16[16,3,256,385]{3,2,0,1:T(8,128)(2,1)} reshape(bf16[16,3,98560]{2,0,1:T(8,128)(2,1)} %slice.57) | data formatting | bytes 18923520 | tf_op jit(solution)/shard_map/while/body/eval_jaxpr/reshape | solution.py:20
  980.6 10.6 tile.28
  999.2 27.5 %reshape.281 = bf16[16,3,256,385]{3,2,0,1:T(8,128)(2,1)} reshape(bf16[16,3,98560]{2,0,1:T(8,128)(2,1)} %slice.57) | data formatting | bytes 18923520 | tf_op jit(solution)/shard_map/while/body/eval_jaxpr/reshape | solution.py:20
  1035.0 10.6 tile.28
  1053.6 27.5 %reshape.281 = bf16[16,3,256,385]{3,2,0,1:T(8,128)(2,1)} reshape(bf16[16,3,98560]{2,0,1:T(8,128)(2,1)} %slice.57) | data formatting | bytes 18923520 | tf_op jit(solution)/shard_map/while/body/eval_jaxpr/reshape | solution.py:20
  1089.4 10.6 tile.28
  1108.1 27.5 %reshape.281 = bf16[16,3,256,385]{3,2,0,1:T(8,128)(2,1)} reshape(bf16[16,3,98560]{2,0,1:T(8,128)(2,1)} %slice.57) | data formatting | bytes 18923520 | tf_op jit(solution)/shard_map/while/body/eval_jaxpr/reshape | solution.py:20
  1143.8 10.6 tile.28
  1162.5 27.5 %reshape.281 = bf16[16,3,256,385]{3,2,0,1:T(8,128)(2,1)} reshape(bf16[16,3,98560]{2,0,1:T(8,128)(2,1)} %slice.57) | data formatting | bytes 18923520 | tf_op jit(solution)/shard_map/while/body/eval_jaxpr/reshape | solution.py:20
  1198.3 10.6 tile.28
  1216.9 27.5 %reshape.281 = bf16[16,3,256,385]{3,2,0,1:T(8,128)(2,1)} reshape(bf16[16,3,98560]{2,0,1:T(8,128)(2,1)} %slice.57) | data formatting | bytes 18923520 | tf_op jit(solution)/shard_map/while/body/eval_jaxpr/reshape | solution.py:20
  (234 shorter events, 343.6 us)
Async XLA Ops:
  0.6 1.2 copy-start
  9.4 11.8 copy-start.8
  9.4 12.5 copy-start.10
  9.4 12.5 copy-start.11
  9.4 78.6 %all-to-all-start = ((bf16[2,128,2,1536]{3,2,0,1:T(2,128)(2,1)}), bf16[2,128,2,1536]{3,2,0,1:T(2,128)(2,1)S(1)}, u32[]{:S(2)}, u32[]{:S(2)}) async-start(bf16[2,128,2,1536]{3,2,0,1:T(2,128)(2,1)} %copy.60), calls=%async_computation | async-start | bytes 3145728 | tf_op jit(solution)/shard_map/all_to_all | solution.py:45
  41.1 20.1 %copy-start.9 = (s32[64,4]{0,1:T(4,128)S(1)}, s32[64,4]{0,1:T(4,128)}, u32[]{:S(2)}) copy-start(s32[64,4]{0,1:T(4,128)} %param.15) | copy-start | bytes 3076
  49.8 31.0 %collective-permute-start = (bf16[64,3,384]{2,0,1:T(8,128)(2,1)S(1)}, bf16[64,3,384]{2,0,1:T(8,128)(2,1)S(1)}, u32[]{:S(2)}, u32[]{:S(2)}) collective-permute-start(bf16[64,3,384]{2,0,1:T(8,128)(2,1)S(1)} %copy.70), channel_id=1, source_target_pairs={{8,0},{16,8},{24,16},{32,24},{40,32},{48,40},{56,48},{64,56},{72,6... | collective-permute-start | bytes 442376 | tf_op jit(solution)/shard_map/ppermute | solution.py:13
  51.3 29.5 %collective-permute-start.1 = (bf16[64,3,384]{2,0,1:T(8,128)(2,1)S(1)}, bf16[64,3,384]{2,0,1:T(8,128)(2,1)S(1)}, u32[]{:S(2)}, u32[]{:S(2)}) collective-permute-start(bf16[64,3,384]{2,0,1:T(8,128)(2,1)S(1)} %copy.70), channel_id=1, source_target_pairs={{0,8},{8,16},{16,24},{24,32},{32,40},{40,48},{48,56},{56,64},{64,7... | collective-permute-start | bytes 442376 | tf_op jit(solution)/shard_map/ppermute | solution.py:13
  55.3 25.6 %collective-permute-start.2 = (bf16[64,3,384]{2,0,1:T(8,128)(2,1)S(1)}, bf16[64,3,384]{2,0,1:T(8,128)(2,1)S(1)}, u32[]{:S(2)}, u32[]{:S(2)}) collective-permute-start(bf16[64,3,384]{2,0,1:T(8,128)(2,1)S(1)} %copy.70), channel_id=1, source_target_pairs={{1,0},{2,1},{3,2},{4,3},{5,4},{6,5},{7,6},{9,8},{10,9},{11,10},{12... | collective-permute-start | bytes 442376 | tf_op jit(solution)/shard_map/ppermute | solution.py:13
  58.5 22.3 %collective-permute-start.3 = (bf16[64,3,384]{2,0,1:T(8,128)(2,1)S(1)}, bf16[64,3,384]{2,0,1:T(8,128)(2,1)S(1)}, u32[]{:S(2)}, u32[]{:S(2)}) collective-permute-start(bf16[64,3,384]{2,0,1:T(8,128)(2,1)S(1)} %copy.70), channel_id=1, source_target_pairs={{0,1},{1,2},{2,3},{3,4},{4,5},{5,6},{6,7},{8,9},{9,10},{10,11},{11... | collective-permute-start | bytes 442376 | tf_op jit(solution)/shard_map/ppermute | solution.py:13
  80.8 0.7 copy-start.4
  80.9 0.7 copy-start.5
  80.9 0.7 copy-start.6
  89.8 2.5 copy-start.2
  201.3 19.8 %copy-start.3 = (bf16[2,3,1536]{2,1,0:T(4,128)(2,1)S(1)}, bf16[2,3,1536]{2,1,0:T(4,128)(2,1)}, u32[]{:S(2)}) copy-start(bf16[2,3,1536]{2,1,0:T(4,128)(2,1)} %copy-done.2) | copy-start | bytes 55300 | tf_op jit(solution)/shard_map/while
  221.3 2.5 copy-start.2
  333.1 19.8 %copy-start.3 = (bf16[2,3,1536]{2,1,0:T(4,128)(2,1)S(1)}, bf16[2,3,1536]{2,1,0:T(4,128)(2,1)}, u32[]{:S(2)}) copy-start(bf16[2,3,1536]{2,1,0:T(4,128)(2,1)} %copy-done.2) | copy-start | bytes 55300 | tf_op jit(solution)/shard_map/while
  365.0 11.2 copy-start.7
  365.0 882.7 %all-to-all-start.1 = ((f32[2,128,2,1024]{3,2,0,1:T(2,128)}), f32[2,128,2,1024]{3,2,0,1:T(2,128)S(1)}, u32[]{:S(2)}, u32[]{:S(2)}) async-start(f32[2,128,2,1024]{3,2,0,1:T(2,128)} %copy.65), calls=%async_computation.1 | async-start | bytes 4194304 | tf_op jit(solution)/shard_map/all_to_all | solution.py:72
  1252.5 4.5 copy-start.1
where the time goes:
time: 1270 us; the launch traced here: 1260 us
  local copies, waits for them, and re-layouts  1010 us (80%)
  other arithmetic  155 us (12%)
  matrix products  44.7 us (4%)
  starting transfers between devices  34.2 us (3%)
    reshape x18, local copies, waits for them, and re-layouts, lagged_rows(): tiled = tiled[..., :rows * (length + 1)].reshape(lead + (rows, length + 1))  463 us
    another operation x48, local copies, waits for them, and re-layouts, lagged_rows(): tiled = jnp.tile(series, (1,) * len(lead) + (rows + 1,))  256 us
    another operation x2, other arithmetic  143 us
    slice x18, local copies, waits for them, and re-layouts, lagged_rows(): tiled = tiled[..., :rows * (length + 1)].reshape(lead + (rows, length + 1))  135 us
    gather x4, local copies, waits for them, and re-layouts, cut(): lax.dynamic_slice(waveforms, (sta, jnp.int32(0), start), (1, 3, size))[0]  46.7 us
    dynamic_update_slice x4, local copies, waits for them, and re-layouts, on_device(): traces = lax.map(correlate, (waveforms, inbox))  39.5 us
    dot_general x16, matrix products, window_block(): jnp.einsum('bct,bctl->bl', mine, lagged, preferred_element_type=jnp.float32)  39 us
    while x14, local copies, waits for them, and re-layouts  34.4 us
  transfers between devices with their start and end apart: 6, of which 0 were waited for; matrix products, arithmetic and copies ran while one was open for 74% of the time, Pallas kernels for 0%

commit v1 on v0

v1 whole, which is shorter than its diff:
```python
import functools
import math

import jax
import jax.numpy as jnp
import ml_dtypes
import numpy as np
from jax import lax
from jax.experimental import pallas as pl
from jax.experimental.pallas import tpu as pltpu
from jax.sharding import PartitionSpec as P

B = 128
TB = 4
SB = 12
LB = 8
ROWS = 6 * SB
DET = 64
WIN = 256
HALF = 64
EPS = 1e-06
CHUNK = 8
F32 = jnp.float32
BF16 = jnp.bfloat16


def parts(matrix):
    high = matrix.astype(ml_dtypes.bfloat16)
    low = (matrix - high.astype(np.float64)).astype(ml_dtypes.bfloat16)
    return high, low


def tables():
    turns = (np.arange(B)[:, None] * (4 * np.arange(B)[None, :] + 1)) % (4 * B)
    angle = turns * (np.pi / (2 * B))
    forward = np.concatenate(parts(np.concatenate([np.cos(angle), -np.sin(angle)], axis=1)), axis=0)
    back = np.concatenate([np.cos(angle.T), -np.sin(angle.T)], axis=0) / B
    inverse = np.concatenate(parts(back), axis=1)
    n, q = np.arange(B)[:, None], np.arange(B)[None, :]
    ends = np.concatenate([n >= q, n < q], axis=1).astype(ml_dtypes.bfloat16)
    return forward, inverse, np.concatenate([ends, ends], axis=0)


def split(value):
    high = value.astype(BF16)
    return high, (value - high.astype(F32)).astype(BF16)


def dot(a, b):
    return jnp.dot(a, b, preferred_element_type=F32)


def up(value, steps):
    return pltpu.roll(value, value.shape[0] - steps, 0)


def transform(rows, forward):
    out = dot(jnp.concatenate([rows, rows], axis=1), forward)
    return out[:, :B], out[:, B:]


def inverse_dot(real, imag, inverse):
    high, low = split(jnp.concatenate([real, imag], axis=1))
    main = dot(high, inverse)
    return main[:, :B] + main[:, B:] + dot(low, inverse[:, :B])


def kernel(sizes, gx_name, gy_name, st, packed, own, partner, data, tiles, fwd, inv, ends, stack, diff,
           xr, xi, wb, rw, pb, zb, sb, xf, pw, lw, lr, li):
    ngx, ngy = sizes
    groups = ngx * ngy
    gx, gy = lax.axis_index(gx_name), lax.axis_index(gy_name)
    me = gx * ngy + gy
    forward = fwd[...]

    def station_step(i, carry):
        x = data[pl.ds(i * CHUNK, CHUNK)].astype(F32)
        real, imag = transform(x.reshape(CHUNK * ROWS, B).astype(BF16), forward)
        at = pl.ds(pl.multiple_of(i * CHUNK * ROWS, CHUNK * ROWS), CHUNK * ROWS)
        xr[at, :] = real + up(imag, 1)
        xi[at, :] = imag - up(real, 1)
        sq = x * x
        third = ROWS // 3
        energy = sq[:, :third] + sq[:, third : 2 * third] + sq[:, 2 * third :]
        high, low = split(energy.reshape(CHUNK * third, B))
        sums = dot(jnp.concatenate([high, low], axis=1), ends[...])
        one = sums[:, :B] + up(sums[:, B:], 1)
        two = one + up(one, 1)
        four = two + up(two, 2)
        rw[pl.ds(pl.multiple_of(i * CHUNK * third, CHUNK * third), CHUNK * third), :] = lax.rsqrt(
            four * (1.0 / (3 * TB * B)) + EPS
        )
        return carry

    lax.fori_loop(0, groups // CHUNK, station_step, 0)

    count = tiles.shape[0]
    square = jnp.zeros((count, B), F32)
    for b in range(3 * TB):
        t = tiles[:, b * B : (b + 1) * B].astype(F32)
        square = square + t * t
    mean = jnp.sum(square, axis=1, keepdims=True) * (1.0 / (3 * TB * B))
    scale = lax.rsqrt((3 * TB * B) * (mean + EPS))
    for b in range(3 * TB):
        real, imag = transform(tiles[:, b * B : (b + 1) * B], forward)
        wb[2 * b] = real * scale
        wb[2 * b + 1] = imag * scale

    slots = st.shape[1]
    templates = st.shape[0]

    def product_step(i, carry):
        for k in range(slots):
            s = st[i, k]
            base = lax.div(s, 2) * ROWS + lax.rem(s, 2) * SB
            row = i * slots + k
            real = jnp.zeros((LB, B), F32)
            imag = jnp.zeros((LB, B), F32)
            for c in range(3):
                for a in range(TB):
                    at = pl.ds(base + c * 2 * SB + a, LB)
                    x_re, x_im = xr[at, :], xi[at, :]
                    w_re = wb[2 * (c * TB + a), pl.ds(row, 1), :]
                    w_im = wb[2 * (c * TB + a) + 1, pl.ds(row, 1), :]
                    real = real + x_re * w_re + x_im * w_im
                    imag = imag + x_im * w_re - x_re * w_im
            at = pl.ds(pl.multiple_of(row * LB, LB), LB)
            pb[at, :B] = real
            pb[at, B:] = imag
        return carry

    lax.fori_loop(0, templates, product_step, 0)

    def back_step(i, carry):
        size = 8 * slots * LB
        part = pb[pl.ds(pl.multiple_of(i * size, size), size), :]
        zb[pl.ds(pl.multiple_of(i * size, size), size), :] = inverse_dot(part[:, :B], part[:, B:], inv[...])
        return carry

    lax.fori_loop(0, templates // 8, back_step, 0)

    def stack_step(i, carry):
        total = jnp.zeros((LB, B), F32)
        for k in range(slots):
            s = st[i, k]
            z = zb[pl.ds(pl.multiple_of((i * slots + k) * LB, LB), LB), :]
            total = total + z * rw[pl.ds(s * SB, LB), :]
        sb[pl.ds(pl.multiple_of(i * LB, LB), LB), :] = total * (1.0 / math.sqrt(slots))
        return carry

    lax.fori_loop(0, templates, stack_step, 0)
    for p in range(LB):
        stack[:, p * B : (p + 1) * B] = sb[pl.ds(p, templates, stride=LB), :]

    moves = ((1, 0), (-1, 0), (0, 1), (0, -1))
    valid = []
    for d, (dx, dy) in enumerate(moves):
        nx, ny = gx + dx, gy + dy
        inside = (nx >= 0) & (nx < ngx) & (ny >= 0) & (ny < ngy)
        valid.append(jnp.where(inside, 1.0, 0.0).astype(F32))
        there = jnp.where(inside, nx * ngy + ny, me)
        xf[d * ROWS : (d + 1) * ROWS] = data[there].astype(F32)
    xf[4 * ROWS : 5 * ROWS] = data[me].astype(F32)
    xf[5 * ROWS :] = jnp.zeros((xf.shape[0] - 5 * ROWS, B), F32)
    lane = lax.broadcasted_iota(jnp.int32, (8, B), 1)

    def window(which, station, start, c):
        block, offset = lax.div(start, B), lax.rem(start, B)
        base = which * ROWS + c * 2 * SB + station * SB + block
        shift = lax.rem(B - offset, B)
        first = pltpu.roll(xf[pl.ds(base, 8), :], shift, 1)
        second = pltpu.roll(xf[pl.ds(base + 1, 8), :], shift, 1)
        return jnp.where(lane < B - offset, first, second)

    def cut_step(e, carry):
        at = pl.ds(pl.multiple_of(e * 4, 4), 8)
        mine = own[e]
        for c in range(3):
            lw[c, at, :] = window(4, lax.div(mine, 2048), lax.rem(mine, 2048), c)
        for d in range(4):
            other = packed[d, partner[e, d]]
            for c in range(3):
                pw[c * 4 + d, at, :] = window(d, lax.div(other, 2048), lax.rem(other, 2048) - HALF, c)
        return carry

    lax.fori_loop(0, DET, cut_step, 0)

    size = 4 * DET
    row_of = lax.rem(lax.broadcasted_iota(jnp.int32, (size, B), 0), 4)
    lane_of = lax.broadcasted_iota(jnp.int32, (size, B), 1)

    def mean_of(square, mask):
        total = jnp.sum(jnp.where(mask, square, 0.0), axis=1, keepdims=True)
        zb[0:size, :] = jnp.broadcast_to(total, (size, B))
        out = zb[pl.ds(0, DET, stride=4), :]
        for r in range(1, 3):
            out = out + zb[pl.ds(r, DET, stride=4), :]
        return out * (1.0 / (3 * WIN))

    square = jnp.zeros((size, B), F32)
    for c in range(3):
        rows = lw[c, 0:size, :]
        square = square + rows * rows
        real, imag = transform(rows.astype(BF16), forward)
        lr[c] = real
        li[c] = imag
    local_scale = lax.rsqrt((3 * WIN) * (mean_of(square, row_of < 2) + EPS))
    centre = ((row_of == 0) & (lane_of >= HALF)) | (row_of == 1) | ((row_of == 2) & (lane_of < HALF))
    for d in range(4):
        square = jnp.zeros((size, B), F32)
        out_re = jnp.zeros((size, B), F32)
        out_im = jnp.zeros((size, B), F32)
        for c in range(3):
            rows = pw[c * 4 + d, 0:size, :]
            square = square + rows * rows
            real, imag = transform(rows.astype(BF16), forward)
            x_re = real + up(imag, 1)
            x_im = imag - up(real, 1)
            w_re, w_im = lr[c], li[c]
            out_re = out_re + x_re * w_re + x_im * w_im
            out_im = out_im + x_im * w_re - x_re * w_im
        piece_scale = lax.rsqrt(mean_of(square, centre) + EPS)
        zb[0:size, :] = inverse_dot(out_re, out_im, inv[...])
        raw = zb[pl.ds(0, DET, stride=4), :] + zb[pl.ds(1, DET, stride=4), :]
        diff[pl.ds(d, DET, stride=4), :] = raw * local_scale * piece_scale * valid[d]


def on_device(waveforms, templates, tpl_stations, det_station, det_time, partner):
    ngx, ngy = lax.axis_size("gx"), lax.axis_size("gy")
    groups = ngx * ngy
    count = templates.shape[0] * templates.shape[1]
    rows = jnp.transpose(waveforms, (1, 0, 2)).reshape(1, ROWS, B)
    data = lax.all_gather(rows, ("gx", "gy"), axis=0, tiled=True)
    own = det_station * 2048 + det_time

    def from_behind(value, axis, steps):
        size = lax.axis_size(axis)
        pairs = [(i, i + steps) for i in range(max(0, -steps), min(size, size - steps))]
        return lax.ppermute(value, axis, pairs)

    packed = jnp.stack([from_behind(own, "gx", -1), from_behind(own, "gx", 1),
                        from_behind(own, "gy", -1), from_behind(own, "gy", 1)])
    packed = jnp.where((packed & 2047) < HALF, HALF, packed)
    forward, inverse, ends = tables()
    smem = pl.BlockSpec(memory_space=pltpu.SMEM)
    vmem = pl.BlockSpec(memory_space=pltpu.VMEM)
    stack, diff = pl.pallas_call(
        functools.partial(kernel, (ngx, ngy), "gx", "gy"),
        out_shape=(
            jax.ShapeDtypeStruct((templates.shape[0], LB * B), F32),
            jax.ShapeDtypeStruct((4 * DET, B), F32),
        ),
        in_specs=[smem] * 4 + [vmem] * 5,
        out_specs=(vmem, vmem),
        scratch_shapes=[
            pltpu.VMEM((groups * ROWS, B), F32),
            pltpu.VMEM((groups * ROWS, B), F32),
            pltpu.VMEM((6 * TB, count, B), F32),
            pltpu.VMEM((groups * 2 * SB, B), F32),
            pltpu.VMEM((count * LB, 2 * B), F32),
            pltpu.VMEM((count * LB, B), F32),
            pltpu.VMEM((templates.shape[0] * LB, B), F32),
            pltpu.VMEM((5 * ROWS + 16, B), F32),
            pltpu.VMEM((12, 4 * DET + 8, B), F32),
            pltpu.VMEM((3, 4 * DET + 8, B), F32),
            pltpu.VMEM((3, 4 * DET, B), F32),
            pltpu.VMEM((3, 4 * DET, B), F32),
        ],
        compiler_params=pltpu.CompilerParams(vmem_limit_bytes=60 * 1024 * 1024),
    )(tpl_stations, packed, own, partner, data, templates.reshape(count, 3 * TB * B),
      jnp.asarray(forward), jnp.asarray(inverse), jnp.asarray(ends))
    return stack, diff.reshape(DET, 4, B)


def solution(mesh):
    return jax.shard_map(
        on_device,
        mesh=mesh,
        in_specs=(
            P(("gx", "gy"), None, None),
            P(("gx", "gy"), None, None),
            P(("gx", "gy"), None),
            P(("gx", "gy")),
            P(("gx", "gy")),
            P(("gx", "gy"), None),
        ),
        out_specs=(P(("gx", "gy"), None), P(("gx", "gy"), None, None)),
        check_vma=False,
    )
```

time: 1270 us -> 112 us (0.09)
  local copies, waits for them, and re-layouts: 1010 us -> 4.08 us
  other arithmetic: 155 us -> 1.27 us
  waiting for transfers between devices: 0.02 us -> 56.7 us
  matrix products: 44.7 us -> 0 us
  Pallas kernels: 0 us -> 24.4 us
  starting transfers between devices: 34.2 us -> 11.3 us
  between operations: 1.18 us -> 14.1 us
    reshape x25 -> x1, local copies, waits for them, and re-layouts: 476 us -> 1.35 us  [on_device(): rows = jnp.transpose(waveforms, (1, 0, 2)).reshape(1, ROWS, B)]
    another operation x49 -> x0, local copies, waits for them, and re-layouts: 257 us -> none  [the longest x48 256 us: lagged_rows(): tiled = jnp.tile(series, (1,) * len(lead) + (rows + 1,))]
    another operation x3 -> x0, other arithmetic: 144 us -> none
    slice x20 -> x0, local copies, waits for them, and re-layouts: 143 us -> none  [the longest x18 135 us: lagged_rows(): tiled = tiled[..., :rows * (length + 1)].reshape(lead + (rows, length + 1))]
    all_gather x0 -> x1, waiting for transfers between devices: none -> 56.4 us  [on_device(): data = lax.all_gather(rows, ('gx', 'gy'), axis=0, tiled=True)]
    gather x7 -> x0, local copies, waits for them, and re-layouts: 51.8 us -> none  [the longest x4 46.7 us: cut(): lax.dynamic_slice(waveforms, (sta, jnp.int32(0), start), (1, 3, size))[0]]
    dot_general x18 -> x0, matrix products: 44.7 us -> none  [the longest x16 39 us: window_block(): jnp.einsum('bct,bctl->bl', mine, lagged, preferred_element_type=jnp.float32)]
    dynamic_update_slice x4 -> x0, local copies, waits for them, and re-layouts: 39.5 us -> none  [on_device(): traces = lax.map(correlate, (waveforms, inbox))]
  transfers between devices with their start and end apart: 6 -> 5, of which waited for: 0 -> 2; matrix products, arithmetic and copies ran while one was open for 74% -> 4% of each run, Pallas kernels for 0% -> 0%
where the time goes in v1:
time: 112 us
  waiting for transfers between devices  56.7 us (51%)
  Pallas kernels  24.4 us (22%)
  between operations  14.1 us (13%)
  starting transfers between devices  11.3 us (10%)
  local copies, waits for them, and re-layouts  4.08 us (4%)
  other arithmetic  1.27 us (1%)
    all_gather x1, waiting for transfers between devices, on_device(): data = lax.all_gather(rows, ('gx', 'gy'), axis=0, tiled=True)  56.4 us
    pallas_call x1, Pallas kernels, on_device(): pl.pallas_call(functools.partial(kernel, (ngx, ngy), 'gx', 'gy'), out_sha...  24.4 us
    ppermute x4, starting transfers between devices, from_behind(): return lax.ppermute(value, axis, pairs)  11.3 us
    unnamed x4, local copies, waits for them, and re-layouts  2.74 us
  transfers between devices with their start and end apart: 5, of which 2 were waited for; matrix products, arithmetic and copies ran while one was open for 4% of the time, Pallas kernels for 0%

profile of v1, /device:TPU:1, one launch (start us, length us, event | category | flops | bytes accessed | tf_op | source)
XLA Modules:
  0.0 111.8 jit_solution(15013123974215486355)
XLA Ops:
  7.2 0.0 all-gather.2.cloned.1.call-start
  7.2 1.3 %reshape.13 = bf16[1,72,128]{2,1,0:T(8,128)(2,1)} reshape(bf16[3,2,1536]{2,1,0:T(2,128)(2,1)} %bitcast.8) | data formatting | bytes 36864 | tf_op jit(solution)/shard_map/reshape | solution.py:232
  8.6 0.0 all-gather.2.cloned.1.call-update
  8.6 0.7 multiply_add_fusion.own
  9.3 0.0 copy-start
  9.3 4.9 %collective-permute-start.3 = (s32[64]{0:T(128)S(1)}, s32[64]{0:T(128)S(1)}, u32[]{:S(2)}, u32[]{:S(2)}) collective-permute-start(s32[64]{0:T(128)S(1)} %multiply_add_fusion.own), channel_id=1, source_target_pairs={{0,1},{1,2},{2,3},{3,4},{4,5},{5,6},{6,7},{8,9},{9,10},{10,11},{11... | collective-permute-start | bytes 776 | tf_op jit(solution)/shard_map/ppermute | solution.py:239
  14.2 1.9 %collective-permute-start.2 = (s32[64]{0:T(128)S(1)}, s32[64]{0:T(128)S(1)}, u32[]{:S(2)}, u32[]{:S(2)}) collective-permute-start(s32[64]{0:T(128)S(1)} %multiply_add_fusion.own), channel_id=1, source_target_pairs={{1,0},{2,1},{3,2},{4,3},{5,4},{6,5},{7,6},{9,8},{10,9},{11,10},{12... | collective-permute-start | bytes 776 | tf_op jit(solution)/shard_map/ppermute | solution.py:239
  16.1 3.1 %collective-permute-start.1 = (s32[64]{0:T(128)S(1)}, s32[64]{0:T(128)S(1)}, u32[]{:S(2)}, u32[]{:S(2)}) collective-permute-start(s32[64]{0:T(128)S(1)} %multiply_add_fusion.own), channel_id=1, source_target_pairs={{0,8},{8,16},{16,24},{24,32},{32,40},{40,48},{48,56},{56,64},{64,7... | collective-permute-start | bytes 776 | tf_op jit(solution)/shard_map/ppermute | solution.py:239
  19.2 1.3 %collective-permute-start = (s32[64]{0:T(128)S(1)}, s32[64]{0:T(128)S(1)}, u32[]{:S(2)}, u32[]{:S(2)}) collective-permute-start(s32[64]{0:T(128)S(1)} %multiply_add_fusion.own), channel_id=1, source_target_pairs={{8,0},{16,8},{24,16},{32,24},{40,32},{48,40},{56,48},{64,56},{72,6... | collective-permute-start | bytes 776 | tf_op jit(solution)/shard_map/ppermute | solution.py:239
  20.5 1.4 %copy.13.st = s32[32,8]{1,0:T(8,128)} copy(s32[32,8]{0,1:T(8,128)} %param.11) | data formatting | bytes 2048 | tf_op args[2]
  21.9 1.4 %copy.14.partner = s32[64,4]{1,0:T(8,128)} copy(s32[64,4]{0,1:T(4,128)} %param.14) | data formatting | bytes 2048 | tf_op args[5]
  23.3 0.0 collective-permute-done.3
  23.3 0.0 collective-permute-done.2
  23.3 0.0 collective-permute-done.1
  23.3 0.2 collective-permute-done
  23.5 0.6 fusion.packed
  24.1 56.4 %all-gather.2.cloned.1.call-done.data = bf16[128,72,128]{2,1,0:T(8,128)(2,1)} async-done(((bf16[1,72,128]{2,1,0:T(8,128)(2,1)}), bf16[128,72,128]{2,1,0:T(8,128)(2,1)}) %all-gather.2.cloned.1.call-update) | async-done | bytes 2359312 | tf_op jit(solution)/shard_map/all_gather | solution.py:233
  80.5 0.0 copy-done
  80.5 24.4 %shard_map.104 = (f32[32,1024]{1,0:T(8,128)}, f32[256,128]{1,0:T(8,128)}) custom-call(s32[32,8]{1,0:T(8,128)} %copy.13.st, s32[4,64]{1,0:T(4,128)} %fusion.packed, s32[64]{0:T(128)} %copy-done, s32[64,4]{1,0:T(8,128)} %copy.14.partner, bf16[128,72,128]{2,1,0:T(8,128)(2,1)} %all-gather.2.cloned.1.call-done.data, bf16[256,1536]{1,0:T(8,128)(2,1)} %bitcast.7, ...), custom_call_target="tpu_custom_call" | custom-call | tf_op jit(solution)/shard_map/pallas_call | solution.py:247
Async XLA Ops:
  7.2 73.4 %all-gather.2.cloned.1.call-start = ((), (), s32[]{:S(2)}) async-start(), calls=%async_computation | async-start | bytes 2377728 | tf_op jit(solution)/shard_map/all_gather | solution.py:233
  9.3 71.3 %copy-start = (s32[64]{0:T(128)}, s32[64]{0:T(128)S(1)}, u32[]{:S(2)}) copy-start(s32[64]{0:T(128)S(1)} %multiply_add_fusion.own) | copy-start | bytes 772
  9.3 14.0 %collective-permute-start.3 = (s32[64]{0:T(128)S(1)}, s32[64]{0:T(128)S(1)}, u32[]{:S(2)}, u32[]{:S(2)}) collective-permute-start(s32[64]{0:T(128)S(1)} %multiply_add_fusion.own), channel_id=1, source_target_pairs={{0,1},{1,2},{2,3},{3,4},{4,5},{5,6},{6,7},{8,9},{9,10},{10,11},{11... | collective-permute-start | bytes 776 | tf_op jit(solution)/shard_map/ppermute | solution.py:239
  14.2 9.1 %collective-permute-start.2 = (s32[64]{0:T(128)S(1)}, s32[64]{0:T(128)S(1)}, u32[]{:S(2)}, u32[]{:S(2)}) collective-permute-start(s32[64]{0:T(128)S(1)} %multiply_add_fusion.own), channel_id=1, source_target_pairs={{1,0},{2,1},{3,2},{4,3},{5,4},{6,5},{7,6},{9,8},{10,9},{11,10},{12... | collective-permute-start | bytes 776 | tf_op jit(solution)/shard_map/ppermute | solution.py:239
  16.1 7.2 %collective-permute-start.1 = (s32[64]{0:T(128)S(1)}, s32[64]{0:T(128)S(1)}, u32[]{:S(2)}, u32[]{:S(2)}) collective-permute-start(s32[64]{0:T(128)S(1)} %multiply_add_fusion.own), channel_id=1, source_target_pairs={{0,8},{8,16},{16,24},{24,32},{32,40},{40,48},{48,56},{56,64},{64,7... | collective-permute-start | bytes 776 | tf_op jit(solution)/shard_map/ppermute | solution.py:239
  19.2 4.3 %collective-permute-start = (s32[64]{0:T(128)S(1)}, s32[64]{0:T(128)S(1)}, u32[]{:S(2)}, u32[]{:S(2)}) collective-permute-start(s32[64]{0:T(128)S(1)} %multiply_add_fusion.own), channel_id=1, source_target_pairs={{8,0},{16,8},{24,16},{32,24},{40,32},{48,40},{56,48},{64,56},{72,6... | collective-permute-start | bytes 776 | tf_op jit(solution)/shard_map/ppermute | solution.py:239
Sparse Core Ops, SparseCore 0:
  11.5 68.9 all-gather.1

commit v2 on v1

--- a/solution.py
+++ b/solution.py
@@ -65,7 +65,96 @@
     return main[:, :B] + main[:, B:] + dot(low, inverse[:, :B])
 
 
-def kernel(sizes, gx_name, gy_name, st, packed, own, partner, data, tiles, fwd, inv, ends, stack, diff,
+def ring_layout(ngx, ngy):
+    nx = math.isqrt(ngx)
+    return {"y": ngx // nx, "x": nx, "z": ngy // 2, "core": 2}
+
+
+ORDERS = (("x", "y", "z"), ("y", "z", "x"), ("z", "x", "y"))
+
+
+def gather_kernel(sizes, wave, stations, times, data, words, rows, mine, send_sem, recv_sem, word_sem):
+    ngx, ngy = sizes
+    dims = ring_layout(ngx, ngy)
+    gx, gy = lax.axis_index("gx"), lax.axis_index("gy")
+    here = {"y": gx // dims["x"], "x": gx % dims["x"], "z": gy // 2, "core": gy % 2}
+
+    def device(coords):
+        return (coords["y"] * dims["x"] + coords["x"], coords["z"] * 2 + coords["core"])
+
+    def moved(axis, steps):
+        return {**here, axis: (here[axis] + steps + dims[axis]) % dims[axis]}
+
+    near = (
+        ((gx + 1) % ngx, gy),
+        ((gx + ngx - 1) % ngx, gy),
+        (gx, (gy + 1) % ngy),
+        (gx, (gy + ngy - 1) % ngy),
+    )
+    peers = [device(moved(axis, r)) for axis in ("x", "y", "z") for r in range(1, dims[axis])]
+    peers = peers + [device(moved("core", 1))] + list(near)
+    barrier = pltpu.get_barrier_semaphore()
+    for peer in peers:
+        pl.semaphore_signal(barrier, inc=1, device_id=peer, device_id_type=pl.DeviceIdType.MESH)
+
+    for c in range(3):
+        value = wave[c].astype(F32)
+        for b in range(SB):
+            rows[c, pl.ds(b, 2, stride=SB), :] = value[:, b * B : (b + 1) * B]
+        data[here["y"], here["x"], here["z"], here["core"], c] = rows[c].astype(BF16)
+    mine[...] = jnp.zeros_like(mine)
+    mine[:, 0:DET] = stations[...] * 2048 + times[...]
+    pl.semaphore_wait(barrier, len(peers))
+
+    started = []
+
+    def send(source, target, to, send_at, recv_at):
+        copy = pltpu.make_async_remote_copy(
+            src_ref=source, dst_ref=target, send_sem=send_at, recv_sem=recv_at,
+            device_id=to, device_id_type=pl.DeviceIdType.MESH)
+        copy.start()
+        started.append(copy)
+        return copy
+
+    def block(coords, whole, c):
+        at = tuple(slice(None) if axis in whole else coords[axis] for axis in ("y", "x", "z", "core"))
+        return data.at[at + (c,)]
+
+    def send_block(coords, whole, c, to, index):
+        ref = block(coords, whole, c)
+        return send(ref, ref, to, send_sem.at[c, index], recv_sem.at[c, index])
+
+    arriving = {c: [] for c in range(3)}
+    for phase in range(3):
+        for c, order in enumerate(ORDERS):
+            for copy in arriving[c]:
+                copy.wait_recv()
+            axis = order[phase]
+            arriving[c] = [
+                send_block(here, order[:phase], c, device(moved(axis, r)), 3 * phase + r - 1)
+                for r in range(1, dims[axis])
+            ]
+        if phase == 0:
+            word_copies = [
+                send(mine, words.at[d ^ 1], near[d], word_sem.at[0, d], word_sem.at[1, d ^ 1]) for d in range(4)
+            ]
+    sibling = device(moved("core", 1))
+    last = []
+    for c, order in enumerate(ORDERS):
+        last.append(send_block(here, order[:2], c, sibling, 9))
+    for r in range(1, 4):
+        for c, order in enumerate(ORDERS):
+            if r < dims[order[2]]:
+                arriving[c][r - 1].wait_recv()
+                came = moved(order[2], -r)
+                last.append(send_block(came, order[:2], c, sibling, 9 + r))
+    for copy in last + word_copies:
+        copy.wait_recv()
+    for copy in started:
+        copy.wait_send()
+
+
+def kernel(sizes, gx_name, gy_name, st, packed, stations, times, partner, data, tiles, fwd, inv, ends, stack, diff,
            xr, xi, wb, rw, pb, zb, sb, xf, pw, lw, lr, li):
     ngx, ngy = sizes
     groups = ngx * ngy
@@ -74,7 +163,7 @@
     forward = fwd[...]
 
     def station_step(i, carry):
-        x = data[pl.ds(i * CHUNK, CHUNK)].astype(F32)
+        x = data[pl.ds(i * CHUNK, CHUNK)].astype(F32).reshape(CHUNK, ROWS, B)
         real, imag = transform(x.reshape(CHUNK * ROWS, B).astype(BF16), forward)
         at = pl.ds(pl.multiple_of(i * CHUNK * ROWS, CHUNK * ROWS), CHUNK * ROWS)
         xr[at, :] = real + up(imag, 1)
@@ -106,12 +195,11 @@
         wb[2 * b] = real * scale
         wb[2 * b + 1] = imag * scale
 
-    slots = st.shape[1]
-    templates = st.shape[0]
+    slots, templates = st.shape
 
     def product_step(i, carry):
         for k in range(slots):
-            s = st[i, k]
+            s = st[k, i]
             base = lax.div(s, 2) * ROWS + lax.rem(s, 2) * SB
             row = i * slots + k
             real = jnp.zeros((LB, B), F32)
@@ -142,7 +230,7 @@
     def stack_step(i, carry):
         total = jnp.zeros((LB, B), F32)
         for k in range(slots):
-            s = st[i, k]
+            s = st[k, i]
             z = zb[pl.ds(pl.multiple_of((i * slots + k) * LB, LB), LB), :]
             total = total + z * rw[pl.ds(s * SB, LB), :]
         sb[pl.ds(pl.multiple_of(i * LB, LB), LB), :] = total * (1.0 / math.sqrt(slots))
@@ -159,8 +247,8 @@
         inside = (nx >= 0) & (nx < ngx) & (ny >= 0) & (ny < ngy)
         valid.append(jnp.where(inside, 1.0, 0.0).astype(F32))
         there = jnp.where(inside, nx * ngy + ny, me)
-        xf[d * ROWS : (d + 1) * ROWS] = data[there].astype(F32)
-    xf[4 * ROWS : 5 * ROWS] = data[me].astype(F32)
+        xf[d * ROWS : (d + 1) * ROWS] = data[there].astype(F32).reshape(ROWS, B)
+    xf[4 * ROWS : 5 * ROWS] = data[me].astype(F32).reshape(ROWS, B)
     xf[5 * ROWS :] = jnp.zeros((xf.shape[0] - 5 * ROWS, B), F32)
     lane = lax.broadcasted_iota(jnp.int32, (8, B), 1)
 
@@ -174,11 +262,11 @@
 
     def cut_step(e, carry):
         at = pl.ds(pl.multiple_of(e * 4, 4), 8)
-        mine = own[e]
+        mine = stations[e] * 2048 + times[e]
         for c in range(3):
             lw[c, at, :] = window(4, lax.div(mine, 2048), lax.rem(mine, 2048), c)
         for d in range(4):
-            other = packed[d, partner[e, d]]
+            other = packed[d, partner[d, e]]
             for c in range(3):
                 pw[c * 4 + d, at, :] = window(d, lax.div(other, 2048), lax.rem(other, 2048) - HALF, c)
         return carry
@@ -229,28 +317,38 @@
     ngx, ngy = lax.axis_size("gx"), lax.axis_size("gy")
     groups = ngx * ngy
     count = templates.shape[0] * templates.shape[1]
-    rows = jnp.transpose(waveforms, (1, 0, 2)).reshape(1, ROWS, B)
-    data = lax.all_gather(rows, ("gx", "gy"), axis=0, tiled=True)
-    own = det_station * 2048 + det_time
-
-    def from_behind(value, axis, steps):
-        size = lax.axis_size(axis)
-        pairs = [(i, i + steps) for i in range(max(0, -steps), min(size, size - steps))]
-        return lax.ppermute(value, axis, pairs)
-
-    packed = jnp.stack([from_behind(own, "gx", -1), from_behind(own, "gx", 1),
-                        from_behind(own, "gy", -1), from_behind(own, "gy", 1)])
-    packed = jnp.where((packed & 2047) < HALF, HALF, packed)
-    forward, inverse, ends = tables()
     smem = pl.BlockSpec(memory_space=pltpu.SMEM)
     vmem = pl.BlockSpec(memory_space=pltpu.VMEM)
+    dims = ring_layout(ngx, ngy)
+    data, words = pl.pallas_call(
+        functools.partial(gather_kernel, (ngx, ngy)),
+        out_shape=(
+            jax.ShapeDtypeStruct((dims["y"], dims["x"], dims["z"], 2, 3, 2 * SB, B), BF16),
+            jax.ShapeDtypeStruct((4, 1, B), jnp.int32),
+        ),
+        in_specs=[vmem] * 3,
+        out_specs=(vmem, vmem),
+        scratch_shapes=[
+            pltpu.VMEM((3, 2 * SB, B), F32),
+            pltpu.VMEM((1, B), jnp.int32),
+            pltpu.SemaphoreType.DMA((3, 13)),
+            pltpu.SemaphoreType.DMA((3, 13)),
+            pltpu.SemaphoreType.DMA((2, 4)),
+        ],
+        compiler_params=pltpu.CompilerParams(
+            collective_id=0, has_side_effects=True, vmem_limit_bytes=16 * 1024 * 1024
+        ),
+    )(jnp.transpose(waveforms, (1, 0, 2)), det_station.reshape(1, DET), det_time.reshape(1, DET))
+    data = data.reshape(groups, 3, 2 * SB, B)
+    packed = words.reshape(4, B)
+    forward, inverse, ends = tables()
     stack, diff = pl.pallas_call(
         functools.partial(kernel, (ngx, ngy), "gx", "gy"),
         out_shape=(
             jax.ShapeDtypeStruct((templates.shape[0], LB * B), F32),
             jax.ShapeDtypeStruct((4 * DET, B), F32),
         ),
-        in_specs=[smem] * 4 + [vmem] * 5,
+        in_specs=[smem] * 5 + [vmem] * 5,
         out_specs=(vmem, vmem),
         scratch_shapes=[
             pltpu.VMEM((groups * ROWS, B), F32),
@@ -267,7 +365,7 @@
             pltpu.VMEM((3, 4 * DET, B), F32),
         ],
         compiler_params=pltpu.CompilerParams(vmem_limit_bytes=60 * 1024 * 1024),
-    )(tpl_stations, packed, own, partner, data, templates.reshape(count, 3 * TB * B),
+    )(tpl_stations.T, packed, det_station, det_time, partner.T, data, templates.reshape(count, 3 * TB * B),
       jnp.asarray(forward), jnp.asarray(inverse), jnp.asarray(ends))
     return stack, diff.reshape(DET, 4, B)
 

time: 112 us -> 53.1 us (0.47)
  waiting for transfers between devices: 56.7 us -> 0 us
  Pallas kernels: 24.4 us -> 48.3 us
  between operations: 14.1 us -> 0.66 us
  starting transfers between devices: 11.3 us -> 0 us
  other arithmetic: 1.27 us -> 0 us
    all_gather x1 -> x0, waiting for transfers between devices: 56.4 us -> none  [on_device(): data = lax.all_gather(rows, ('gx', 'gy'), axis=0, tiled=True)]
    pallas_call x0 -> x1, Pallas kernels: none -> 24.1 us  [on_device(): pl.pallas_call(functools.partial(gather_kernel, (ngx, ngy)), out_shape=(j...]
    ppermute x4 -> x0, starting transfers between devices: 11.3 us -> none  [from_behind(): return lax.ppermute(value, axis, pairs)]
    reshape x1 -> x0, local copies, waits for them, and re-layouts: 1.35 us -> none  [on_device(): rows = jnp.transpose(waveforms, (1, 0, 2)).reshape(1, ROWS, B)]
    unnamed x4 -> x10, local copies, waits for them, and re-layouts: 2.74 us -> 3.99 us
  transfers between devices with their start and end apart: 5 -> 0, of which waited for: 2 -> 0; matrix products, arithmetic and copies ran while one was open for 4% -> 0% of each run, Pallas kernels for 0% -> 0%
where the time goes in v2:
time: 53.1 us; the launch traced here: 52.9 us
  Pallas kernels  48.3 us (91%)
  local copies, waits for them, and re-layouts  3.99 us (8%)
  between operations  0.66 us (1%)
    pallas_call x1, Pallas kernels, on_device(): pl.pallas_call(functools.partial(kernel, (ngx, ngy), 'gx', 'gy'), out_sha...  24.2 us
    pallas_call x1, Pallas kernels, on_device(): pl.pallas_call(functools.partial(gather_kernel, (ngx, ngy)), out_shape=(j...  24.1 us
    unnamed x10, local copies, waits for them, and re-layouts  3.99 us

profile of v2, /device:TPU:1, one launch (start us, length us, event | category | flops | bytes accessed | tf_op | source)
XLA Modules:
  0.0 52.9 jit_solution(10312548987371768911)
XLA Ops:
  0.6 0.0 copy-start.1
  0.6 0.7 %copy-done.1 = bf16[2,3,1536]{2,0,1:T(2,128)(2,1)S(1)} copy-done((bf16[2,3,1536]{2,0,1:T(2,128)(2,1)S(1)}, bf16[2,3,1536]{2,0,1:T(2,128)(2,1)}, u32[]{:S(2)}) %copy-start.1) | copy-done | bytes 18456
  1.4 0.0 copy-start.3
  1.4 0.7 %copy-done.3 = s32[64]{0:T(128)S(1)} copy-done((s32[64]{0:T(128)S(1)}, s32[64]{0:T(128)}, u32[]{:S(2)}) %copy-start.3) | copy-done | bytes 280
  2.0 0.0 copy-start.4
  2.0 0.7 %copy-done.4 = s32[64]{0:T(128)S(1)} copy-done((s32[64]{0:T(128)S(1)}, s32[64]{0:T(128)}, u32[]{:S(2)}) %copy-start.4) | copy-done | bytes 280
  2.7 24.1 %shard_map.104 = (bf16[4,4,4,2,3,24,128]{6,5,4,3,2,1,0:T(8,128)(2,1)S(1)}, s32[4,1,128]{2,1,0:T(1,128)S(1)}) custom-call(bf16[3,2,1536]{2,1,0:T(2,128)(2,1)S(1)} %bitcast.10, s32[1,64]{1,0:T(1,128)S(1)} %bitcast.12, s32[1,64]{1,0:T(1,128)S(1)} %bitcast.13), custom_call_target="tpu_custom_call" | custom-call | tf_op jit(solution)/shard_map/pallas_call | solution.py:323
  26.7 0.0 copy-start
  26.7 1.4 %copy-done = bf16[4,4,4,2,3,24,128]{6,5,4,3,2,1,0:T(8,128)(2,1)} copy-done((bf16[4,4,4,2,3,24,128]{6,5,4,3,2,1,0:T(8,128)(2,1)}, bf16[4,4,4,2,3,24,128]{6,5,4,3,2,1,0:T(8,128)(2,1)S(1)}, u32[]{:S(2)}) %copy-start) | copy-done | bytes 2359320
  28.1 0.0 copy-start.2
  28.1 0.6 %copy-done.2 = s32[4,1,128]{2,1,0:T(1,128)} copy-done((s32[4,1,128]{2,1,0:T(1,128)}, s32[4,1,128]{2,1,0:T(1,128)S(1)}, u32[]{:S(2)}) %copy-start.2) | copy-done | bytes 2072
  28.7 24.2 %shard_map.105 = (f32[32,1024]{1,0:T(8,128)}, f32[256,128]{1,0:T(8,128)}) custom-call(s32[8,32]{1,0:T(8,128)} %bitcast.15, s32[4,128]{1,0:T(4,128)} %bitcast.11, s32[64]{0:T(128)} %stations.1, s32[64]{0:T(128)} %times.1, s32[4,64]{1,0:T(4,128)} %bitcast.16, bf16[128,3,24,128]{3,2,1,0:T(8,128)(2,1)} %bitcast.9, bf16[256,1536]{1,0:T(8,128)(2,1)} %bitcast.14, ...), custom_call_target="tpu_custom_call" | custom-call | tf_op jit(solution)/shard_map/pallas_call | solution.py:345
Async XLA Ops:
  0.6 0.7 %copy-start.1 = (bf16[2,3,1536]{2,0,1:T(2,128)(2,1)S(1)}, bf16[2,3,1536]{2,0,1:T(2,128)(2,1)}, u32[]{:S(2)}) copy-start(bf16[2,3,1536]{2,0,1:T(2,128)(2,1)} %param.9) | copy-start | bytes 55300
  1.4 0.7 %copy-start.3 = (s32[64]{0:T(128)S(1)}, s32[64]{0:T(128)}, u32[]{:S(2)}) copy-start(s32[64]{0:T(128)} %stations.1) | copy-start | bytes 772
  2.0 0.7 %copy-start.4 = (s32[64]{0:T(128)S(1)}, s32[64]{0:T(128)}, u32[]{:S(2)}) copy-start(s32[64]{0:T(128)} %times.1) | copy-start | bytes 772
  26.7 1.4 %copy-start = (bf16[4,4,4,2,3,24,128]{6,5,4,3,2,1,0:T(8,128)(2,1)}, bf16[4,4,4,2,3,24,128]{6,5,4,3,2,1,0:T(8,128)(2,1)S(1)}, u32[]{:S(2)}) copy-start(bf16[4,4,4,2,3,24,128]{6,5,4,3,2,1,0:T(8,128)(2,1)S(1)} %get-tuple-element.7) | copy-start | bytes 7077892
  28.1 0.6 %copy-start.2 = (s32[4,1,128]{2,1,0:T(1,128)}, s32[4,1,128]{2,1,0:T(1,128)S(1)}, u32[]{:S(2)}) copy-start(s32[4,1,128]{2,1,0:T(1,128)S(1)} %get-tuple-element.6) | copy-start | bytes 6148

commit v3 on v1

v3 whole, which is shorter than its diff:
```python
import functools
import math

import jax
import jax.numpy as jnp
import ml_dtypes
import numpy as np
from jax import lax
from jax.experimental import pallas as pl
from jax.experimental.pallas import tpu as pltpu
from jax.sharding import PartitionSpec as P

B = 128
TB = 4
SB = 12
LB = 8
ROWS = 6 * SB
DET = 64
WIN = 256
HALF = 64
EPS = 1e-06
CHUNK = 8
F32 = jnp.float32
BF16 = jnp.bfloat16


def parts(matrix):
    high = matrix.astype(ml_dtypes.bfloat16)
    low = (matrix - high.astype(np.float64)).astype(ml_dtypes.bfloat16)
    return high, low


def tables():
    turns = (np.arange(B)[:, None] * (4 * np.arange(B)[None, :] + 1)) % (4 * B)
    angle = turns * (np.pi / (2 * B))
    forward = np.concatenate(parts(np.concatenate([np.cos(angle), -np.sin(angle)], axis=1)), axis=0)
    back = np.concatenate([np.cos(angle.T), -np.sin(angle.T)], axis=0) / B
    inverse = np.concatenate(parts(back), axis=1)
    n, q = np.arange(B)[:, None], np.arange(B)[None, :]
    ends = np.concatenate([n >= q, n < q], axis=1).astype(ml_dtypes.bfloat16)
    return forward, inverse, np.concatenate([ends, ends], axis=0)


def split(value):
    high = value.astype(BF16)
    return high, (value - high.astype(F32)).astype(BF16)


def dot(a, b):
    return jnp.dot(a, b, preferred_element_type=F32)


def up(value, steps):
    return pltpu.roll(value, value.shape[0] - steps, 0)


def transform(rows, forward):
    out = dot(jnp.concatenate([rows, rows], axis=1), forward)
    return out[:, :B], out[:, B:]


def inverse_dot(real, imag, inverse):
    high, low = split(jnp.concatenate([real, imag], axis=1))
    main = dot(high, inverse)
    return main[:, :B] + main[:, B:] + dot(low, inverse[:, :B])


def ring_layout(ngx, ngy):
    nx = math.isqrt(ngx)
    return {"y": ngx // nx, "x": nx, "z": ngy // 2, "core": 2}


ORDERS = (("x", "y", "z"), ("y", "z", "x"), ("z", "x", "y"))


def kernel(sizes, st, stations, times, partner, wave_in, station_in, time_in, tiles_in, fwd_in, inv_in, ends_in, stack, diff,
           data, near_data, wave, tiles, fwd, inv, ends, rows, station_row, time_row, mine, words, packed,
           xr, xi, wb, rw, pb, sb, xf, pw, lw, lr, li, lq, pq, er, ei, gr, gi,
           send_sem, recv_sem, near_sem, word_sem, load_sem):
    ngx, ngy = sizes
    dims = ring_layout(ngx, ngy)
    groups = ngx * ngy
    gx, gy = lax.axis_index("gx"), lax.axis_index("gy")
    here = {"y": gx // dims["x"], "x": gx % dims["x"], "z": gy // 2, "core": gy % 2}
    mesh_id = pl.DeviceIdType.MESH
    third = 2 * SB

    def device(coords):
        return (coords["y"] * dims["x"] + coords["x"], coords["z"] * 2 + coords["core"])

    def linear(coords):
        return ((coords["y"] * dims["x"] + coords["x"]) * dims["z"] + coords["z"]) * 2 + coords["core"]

    def moved(axis, steps):
        return {**here, axis: (here[axis] + steps + dims[axis]) % dims[axis]}

    loads = []
    for i, (source, target) in enumerate(
        ((wave_in, wave), (station_in, station_row), (time_in, time_row), (fwd_in, fwd), (tiles_in, tiles),
         (inv_in, inv), (ends_in, ends))
    ):
        copy = pltpu.make_async_copy(source, target, load_sem.at[i])
        copy.start()
        loads.append(copy)

    near = (
        ((gx + 1) % ngx, gy),
        ((gx + ngx - 1) % ngx, gy),
        (gx, (gy + 1) % ngy),
        (gx, (gy + ngy - 1) % ngy),
    )
    sibling = device(moved("core", 1))
    peers = [device(moved(axis, r)) for axis in ("x", "y", "z") for r in range(1, dims[axis])]
    peers = peers + [sibling] + list(near)
    barrier = pltpu.get_barrier_semaphore()
    for peer in peers:
        pl.semaphore_signal(barrier, inc=1, device_id=peer, device_id_type=mesh_id)

    loads[0].wait()
    for c in range(3):
        value = wave[c].astype(F32)
        for b in range(SB):
            rows[c, pl.ds(b, 2, stride=SB), :] = value[:, b * B : (b + 1) * B]
        data[here["y"], here["x"], here["z"], here["core"], c] = rows[c].astype(BF16)
    loads[1].wait()
    loads[2].wait()
    mine[...] = jnp.zeros_like(mine)
    mine[:, 0:DET] = station_row[...] * 2048 + time_row[...]
    pl.semaphore_wait(barrier, len(peers))

    def send(source, target, to, send_at, recv_at):
        return pltpu.make_async_remote_copy(
            src_ref=source, dst_ref=target, send_sem=send_at, recv_sem=recv_at, device_id=to, device_id_type=mesh_id)

    def place(coords, whole):
        return tuple(slice(None) if axis in whole else coords[axis] for axis in ("y", "x", "z", "core"))

    def block_copy(coords, whole, c, to, index):
        ref = data.at[place(coords, whole) + (c,)]
        return send(ref, ref, to, send_sem.at[c, index], recv_sem.at[c, index])

    def phase_copy(c, phase, r):
        order = ORDERS[c]
        return block_copy(here, order[:phase], c, device(moved(order[phase], r)), 3 * phase + r - 1)

    def steps(c, phase):
        count = dims[ORDERS[c][phase]]
        return [r for r in (1, 3, 2) if r < count]

    def start_phase(phase):
        for c in range(3):
            if phase:
                for r in steps(c, phase - 1):
                    phase_copy(c, phase - 1, r).wait_recv()
            for r in steps(c, phase):
                phase_copy(c, phase, r).start()

    def plane_copy(c, r):
        return block_copy(moved(ORDERS[c][2], -r), ORDERS[c][:2], c, sibling, 9 + r)

    start_phase(0)
    own_block = data.at[place(here, ()) + (slice(None),)]
    near_copies = []
    for d in range(4):
        near_copies.append(send(mine, words.at[d ^ 1], near[d], word_sem.at[0, d], word_sem.at[1, d ^ 1]))
        near_copies.append(send(own_block, near_data.at[d ^ 1], near[d], near_sem.at[0, d], near_sem.at[1, d ^ 1]))
    for copy in near_copies:
        copy.start()

    for copy in loads[3:]:
        copy.wait()
    forward = fwd[...]
    count = tiles.shape[0]
    square = jnp.zeros((count, B), F32)
    for b in range(3 * TB):
        t = tiles[:, b * B : (b + 1) * B].astype(F32)
        square = square + t * t
    mean = jnp.sum(square, axis=1, keepdims=True) * (1.0 / (3 * TB * B))
    scale = lax.rsqrt((3 * TB * B) * (mean + EPS))
    for b in range(3 * TB):
        real, imag = transform(tiles[:, b * B : (b + 1) * B], forward)
        wb[2 * b] = real * scale
        wb[2 * b + 1] = imag * scale

    start_phase(1)

    moves = ((1, 0), (-1, 0), (0, 1), (0, -1))
    span = 2 * SB
    xf[...] = jnp.zeros_like(xf)
    flat = xf.reshape(8 * xf.shape[0], B)
    valid = []
    for copy in near_copies:
        copy.wait_recv()
    to_scalars = pltpu.make_async_copy(words, packed, load_sem.at[7])
    to_scalars.start()
    for d, (dx, dy) in enumerate(moves + ((0, 0),)):
        nx, ny = gx + dx, gy + dy
        inside = (nx >= 0) & (nx < ngx) & (ny >= 0) & (ny < ngy)
        valid.append(jnp.where(inside, 1.0, 0.0).astype(F32))
        x = (near_data[d] if d < 4 else data[place(here, ())]).astype(F32)
        for c in range(3):
            flat[pl.ds((1 + d * span) * 8 + c, span, stride=8), :] = x[c]
            flat[pl.ds(d * span * 8 + 4 + c, span, stride=8), :] = x[c]
    to_scalars.wait()
    lane = lax.broadcasted_iota(jnp.int32, (8, B), 1)
    upper = lax.broadcasted_iota(jnp.int32, (8, B), 0) < 4
    mask_first = jnp.where(upper & (lane < HALF), 0.0, 1.0).astype(F32)
    mask_last = jnp.where(upper | (lane >= HALF), 0.0, 1.0).astype(F32)

    def window(which, station, start, blocks):
        block, offset = lax.shift_right_logical(start, 7), lax.bitwise_and(start, B - 1)
        base = 1 + which * span + station * SB + block
        shift = lax.bitwise_and(B - offset, B - 1)
        inner = lane < B - offset
        turned = [pltpu.roll(xf[base + j], shift, 1) for j in range(blocks)]
        return [jnp.where(inner, turned[j], turned[j + 1]) for j in range(blocks - 1)]

    def cut_step(e, carry):
        at = pl.ds(pl.multiple_of(e * 8, 8), 8)
        (first,) = window(4, stations[e], times[e], 2)
        lw[at, :] = first
        lq[at, :] = first * first
        for d in range(4):
            word = packed[d, 0, partner[d, e]]
            start = jnp.maximum(lax.bitwise_and(word, 2047) - HALF, 0)
            first, second = window(d, lax.shift_right_logical(word, 11), start, 3)
            pw[d, pl.ds(pl.multiple_of(e * 12, 4), 8), :] = first
            pw[d, pl.ds(pl.multiple_of(e * 12 + 4, 4), 8), :] = second
            pq[d, at, :] = first * first * mask_first + second * second * mask_last
        return carry

    lax.fori_loop(0, DET, cut_step, 0, unroll=4)

    start_phase(2)
    for c in range(3):
        plane_copy(c, 0).start()

    lr[...], li[...] = transform(lw[...].astype(BF16), forward)
    for d in range(4):
        er[d], ei[d] = transform(pw[d].astype(BF16), forward)

    def pair_step(e, carry):
        at = pl.ds(pl.multiple_of(e * 8, 8), 8)
        low, high = pl.ds(pl.multiple_of(e * 12, 4), 8), pl.ds(pl.multiple_of(e * 12 + 4, 4), 8)
        w_re, w_im = lr[at, :], li[at, :]
        for d in range(4):
            x_re = er[d, low, :] + ei[d, high, :]
            x_im = ei[d, low, :] - er[d, high, :]
            gr[d, at, :] = x_re * w_re + x_im * w_im
            gi[d, at, :] = x_im * w_re - x_re * w_im
        return carry

    lax.fori_loop(0, DET, pair_step, 0, unroll=2)

    def gathered(ref, *lead):
        out = ref[lead + (pl.ds(0, DET, stride=8),)]
        for r in range(1, 8):
            out = out + ref[lead + (pl.ds(r, DET, stride=8),)]
        return out

    def mean_of(ref, *lead):
        return jnp.sum(gathered(ref, *lead), axis=1, keepdims=True) * (1.0 / (3 * WIN))

    local_scale = lax.rsqrt((3 * WIN) * (mean_of(lq) + EPS))
    for d in range(4):
        raw = inverse_dot(gathered(gr, d), gathered(gi, d), inv[...])
        scale = local_scale * lax.rsqrt(mean_of(pq, d) + EPS) * valid[d]
        diff[pl.ds(d, DET, stride=4), :] = raw * scale

    def transform_plane(c, coords):
        order = ORDERS[c]
        inner = [axis for axis in ("y", "x", "z") if axis in order[:2]]
        size = dims[inner[0]] * dims[inner[1]]
        x = data[place(coords, order[:2]) + (c,)].astype(F32).reshape(size * third, B)
        real, imag = transform(x.astype(BF16), forward)
        w_re, w_im = real + up(imag, 1), imag - up(real, 1)
        for i in range(size):
            full = {**coords, inner[0]: i // dims[inner[1]], inner[1]: i % dims[inner[1]]}
            for sta in range(2):
                at = 2 * (c * groups + linear(full)) + sta
                begin = i * third + sta * SB
                xr[at, 0:SB] = w_re[begin : begin + SB]
                xi[at, 0:SB] = w_im[begin : begin + SB]

    def energy(core):
        def step(y, carry):
            size = dims["x"] * dims["z"]
            x = data[y, :, :, core].astype(F32)
            sq = x * x
            total = (sq[:, :, 0] + sq[:, :, 1] + sq[:, :, 2]).reshape(size * third, B)
            high, low = split(total)
            sums = dot(jnp.concatenate([high, low], axis=1), ends[...])
            one = sums[:, :B] + up(sums[:, B:], 1)
            two = one + up(one, 1)
            four = two + up(two, 2)
            out = lax.rsqrt(four * (1.0 / (3 * TB * B)) + EPS)
            for i in range(size):
                full = {"y": y, "x": i // dims["z"], "z": i % dims["z"], "core": core}
                for sta in range(2):
                    begin = i * third + sta * SB
                    rw[2 * linear(full) + sta] = out[begin : begin + LB]
            return carry

        lax.fori_loop(0, dims["y"], step, 0)

    side = dims["z"]

    def turn(o):
        return o + (o // 2) * (1 - 2 * (o % 2))

    def own_step(o, carry):
        r = turn(o)
        for c in range(3):
            @pl.when(o > 0)
            def _():
                block_copy(here, ORDERS[c][:2], c, device(moved(ORDERS[c][2], r)), 5 + r).wait_recv()
                plane_copy(c, r).start()
        for c in range(3):
            transform_plane(c, moved(ORDERS[c][2], -r))
        return carry

    lax.fori_loop(0, side, own_step, 0)
    energy(here["core"])

    def other_step(o, carry):
        r = turn(o)
        for c in range(3):
            plane_copy(c, r).wait_recv()
        for c in range(3):
            transform_plane(c, {**moved(ORDERS[c][2], -r), "core": 1 - here["core"]})
        return carry

    lax.fori_loop(0, side, other_step, 0)
    energy(1 - here["core"])

    slots, templates = st.shape

    def product_step(i, carry):
        for k in range(slots):
            s = st[k, i]
            row = i * slots + k
            real = jnp.zeros((LB, B), F32)
            imag = jnp.zeros((LB, B), F32)
            for c in range(3):
                all_re, all_im = xr[s + 2 * c * groups], xi[s + 2 * c * groups]
                for a in range(TB):
                    x_re, x_im = all_re[a : a + LB], all_im[a : a + LB]
                    w_re = wb[2 * (c * TB + a), pl.ds(row, 1), :]
                    w_im = wb[2 * (c * TB + a) + 1, pl.ds(row, 1), :]
                    real = real + x_re * w_re + x_im * w_im
                    imag = imag + x_im * w_re - x_re * w_im
            at = pl.ds(pl.multiple_of(row * LB, LB), LB)
            pb[at, :B] = real
            pb[at, B:] = imag
        return carry

    lax.fori_loop(0, templates, product_step, 0)
    group = 2

    def back_step(i, carry):
        size = group * slots * LB
        part = pb[pl.ds(pl.multiple_of(i * size, size), size), :]
        z = inverse_dot(part[:, :B], part[:, B:], inv[...])
        for j in range(group):
            total = jnp.zeros((LB, B), F32)
            for k in range(slots):
                s = st[k, i * group + j]
                row = (j * slots + k) * LB
                total = total + z[row : row + LB] * rw[s]
            sb[pl.ds(pl.multiple_of((i * group + j) * LB, LB), LB), :] = total * (1.0 / math.sqrt(slots))
        return carry

    lax.fori_loop(0, templates // group, back_step, 0, unroll=2)
    for p in range(LB):
        stack[:, p * B : (p + 1) * B] = sb[pl.ds(p, templates, stride=LB), :]

    for copy in near_copies:
        copy.wait_send()
    for c in range(3):
        for phase in range(3):
            for r in steps(c, phase):
                phase_copy(c, phase, r).wait_send()
        for r in range(side):
            plane_copy(c, r).wait_send()


def on_device(waveforms, templates, tpl_stations, det_station, det_time, partner):
    ngx, ngy = lax.axis_size("gx"), lax.axis_size("gy")
    groups = ngx * ngy
    count = templates.shape[0] * templates.shape[1]
    forward, inverse, ends = tables()
    smem = pl.BlockSpec(memory_space=pltpu.SMEM)
    vmem = pl.BlockSpec(memory_space=pltpu.VMEM)
    anywhere = pl.BlockSpec(memory_space=pl.ANY)
    dims = ring_layout(ngx, ngy)
    ntpl = templates.shape[0]

    def floats(*shape):
        return pltpu.VMEM(shape, F32)

    def halves(*shape):
        return pltpu.VMEM(shape, BF16)

    def ints(*shape):
        return pltpu.VMEM(shape, jnp.int32)

    stack, diff = pl.pallas_call(
        functools.partial(kernel, (ngx, ngy)),
        out_shape=(
            jax.ShapeDtypeStruct((ntpl, LB * B), F32),
            jax.ShapeDtypeStruct((4 * DET, B), F32),
        ),
        in_specs=[smem] * 4 + [anywhere] * 7,
        out_specs=(vmem, vmem),
        scratch_shapes=[
            halves(dims["y"], dims["x"], dims["z"], 2, 3, 2 * SB, B),
            halves(4, 3, 2 * SB, B),
            halves(3, 2, SB * B),
            halves(count, 3 * TB * B),
            halves(2 * B, 2 * B),
            halves(2 * B, 2 * B),
            halves(2 * B, 2 * B),
            floats(3, 2 * SB, B),
            ints(1, DET),
            ints(1, DET),
            ints(1, B),
            ints(4, 1, B),
            pltpu.SMEM((4, 1, B), jnp.int32),
            floats(groups * 6, 16, B),
            floats(groups * 6, 16, B),
            floats(6 * TB, count, B),
            floats(groups * 2, LB, B),
            floats(count * LB, 2 * B),
            floats(ntpl * LB, B),
            floats(10 * SB + 4, 8, B),
            floats(4, 12 * DET, B),
            floats(8 * DET, B),
            floats(8 * DET, B),
            floats(8 * DET, B),
            floats(8 * DET, B),
            floats(4, 8 * DET, B),
            floats(4, 12 * DET, B),
            floats(4, 12 * DET, B),
            floats(4, 8 * DET, B),
            floats(4, 8 * DET, B),
            pltpu.SemaphoreType.DMA((3, 13)),
            pltpu.SemaphoreType.DMA((3, 13)),
            pltpu.SemaphoreType.DMA((2, 4)),
            pltpu.SemaphoreType.DMA((2, 4)),
            pltpu.SemaphoreType.DMA((8,)),
        ],
        compiler_params=pltpu.CompilerParams(
            collective_id=0, has_side_effects=True, vmem_limit_bytes=60 * 1024 * 1024
        ),
    )(tpl_stations.T, det_station, det_time, partner.T, jnp.transpose(waveforms, (1, 0, 2)),
      det_station.reshape(1, DET), det_time.reshape(1, DET), templates.reshape(count, 3 * TB * B),
      jnp.asarray(forward), jnp.asarray(inverse), jnp.asarray(ends))
    return stack, diff.reshape(DET, 4, B)


def solution(mesh):
    return jax.shard_map(
        on_device,
        mesh=mesh,
        in_specs=(
            P(("gx", "gy"), None, None),
            P(("gx", "gy"), None, None),
            P(("gx", "gy"), None),
            P(("gx", "gy")),
            P(("gx", "gy")),
            P(("gx", "gy"), None),
        ),
        out_specs=(P(("gx", "gy"), None), P(("gx", "gy"), None, None)),
        check_vma=False,
    )
```

time: 112 us -> 41.7 us (0.37)
  waiting for transfers between devices: 56.7 us -> 0 us
  Pallas kernels: 24.4 us -> 38.6 us
  between operations: 14.1 us -> 0.65 us
  starting transfers between devices: 11.3 us -> 0 us
  local copies, waits for them, and re-layouts: 4.08 us -> 2.26 us
  other arithmetic: 1.27 us -> 0 us
    all_gather x1 -> x0, waiting for transfers between devices: 56.4 us -> none  [on_device(): data = lax.all_gather(rows, ('gx', 'gy'), axis=0, tiled=True)]
    pallas_call x1, Pallas kernels: 24.4 us -> 38.6 us  [on_device(): pl.pallas_call(functools.partial(kernel, (ngx, ngy)), out_shape=(jax.Shap...]
    ppermute x4 -> x0, starting transfers between devices: 11.3 us -> none  [from_behind(): return lax.ppermute(value, axis, pairs)]
    reshape x1 -> x0, local copies, waits for them, and re-layouts: 1.35 us -> none  [on_device(): rows = jnp.transpose(waveforms, (1, 0, 2)).reshape(1, ROWS, B)]
  transfers between devices with their start and end apart: 5 -> 0, of which waited for: 2 -> 0; matrix products, arithmetic and copies ran while one was open for 4% -> 0% of each run, Pallas kernels for 0% -> 0%
where the time goes in v3:
time: 41.7 us; the launch traced here: 41.5 us
  Pallas kernels  38.6 us (93%)
  local copies, waits for them, and re-layouts  2.26 us (5%)
  between operations  0.65 us (2%)
    pallas_call x1, Pallas kernels, on_device(): pl.pallas_call(functools.partial(kernel, (ngx, ngy)), out_shape=(jax.Shap...  38.6 us
    unnamed x4, local copies, waits for them, and re-layouts  2.26 us

profile of v3, /device:TPU:1, one launch (start us, length us, event | category | flops | bytes accessed | tf_op | source)
XLA Modules:
  0.0 41.5 jit_solution(10272198415399172684)
XLA Ops:
  0.6 38.6 %shard_map.104 = (f32[32,1024]{1,0:T(8,128)}, f32[256,128]{1,0:T(8,128)}) custom-call(s32[8,32]{1,0:T(8,128)} %bitcast.10, s32[64]{0:T(128)} %stations.1, s32[64]{0:T(128)} %times.1, s32[4,64]{1,0:T(4,128)} %bitcast.11, bf16[3,2,1536]{2,1,0:T(2,128)(2,1)} %bitcast.9, s32[1,64]{1,0:T(1,128)} %bitcast.12, s32[1,64]{1,0:T(1,128)} %bitcast.13, ...), custom_call_target="tpu_custom_call" | custom-call | tf_op jit(solution)/shard_map/pallas_call | solution.py:407
  39.2 0.0 copy-start
  39.2 1.6 %copy.13 = f32[32,1024]{1,0:T(8,128)} copy(f32[32,1024]{1,0:T(8,128)} %get-tuple-element.8) | data formatting | bytes 262144
  40.8 0.0 copy-done
  40.9 0.7 %copy.14 = f32[64,4,128]{2,1,0:T(4,128)} copy(f32[64,4,128]{2,1,0:T(4,128)S(1)} %bitcast.8) | data formatting | bytes 262144
Async XLA Ops:
  39.2 1.6 %copy-start = (f32[256,128]{1,0:T(8,128)S(1)}, f32[256,128]{1,0:T(8,128)}, u32[]{:S(2)}) copy-start(f32[256,128]{1,0:T(8,128)} %get-tuple-element.5) | copy-start | bytes 393220

commit v4 on v3

--- a/solution.py
+++ b/solution.py
@@ -342,9 +342,9 @@
             real = jnp.zeros((LB, B), F32)
             imag = jnp.zeros((LB, B), F32)
             for c in range(3):
-                all_re, all_im = xr[s + 2 * c * groups], xi[s + 2 * c * groups]
+                at = s + 2 * c * groups
                 for a in range(TB):
-                    x_re, x_im = all_re[a : a + LB], all_im[a : a + LB]
+                    x_re, x_im = xr[at, a : a + LB], xi[at, a : a + LB]
                     w_re = wb[2 * (c * TB + a), pl.ds(row, 1), :]
                     w_im = wb[2 * (c * TB + a) + 1, pl.ds(row, 1), :]
                     real = real + x_re * w_re + x_im * w_im

time: 41.7 us -> 38.1 us (0.914)
  Pallas kernels: 38.6 us -> 35 us
    pallas_call x1, Pallas kernels: 38.6 us -> 35 us  [on_device(): pl.pallas_call(functools.partial(kernel, (ngx, ngy)), out_shape=(jax.Shap...]
where the time goes in v4:
time: 38.1 us; the launch traced here: 37.9 us
  Pallas kernels  35 us (92%)
  local copies, waits for them, and re-layouts  2.26 us (6%)
  between operations  0.65 us (2%)
    pallas_call x1, Pallas kernels, on_device(): pl.pallas_call(functools.partial(kernel, (ngx, ngy)), out_shape=(jax.Shap...  35 us
    unnamed x4, local copies, waits for them, and re-layouts  2.26 us

profile of v4, /device:TPU:1, one launch (start us, length us, event | category | flops | bytes accessed | tf_op | source)
XLA Modules:
  0.0 37.9 jit_solution(3015075659175946511)
XLA Ops:
  0.6 35.0 %shard_map.104 = (f32[32,1024]{1,0:T(8,128)}, f32[256,128]{1,0:T(8,128)}) custom-call(s32[8,32]{1,0:T(8,128)} %bitcast.10, s32[64]{0:T(128)} %stations.1, s32[64]{0:T(128)} %times.1, s32[4,64]{1,0:T(4,128)} %bitcast.11, bf16[3,2,1536]{2,1,0:T(2,128)(2,1)} %bitcast.9, s32[1,64]{1,0:T(1,128)} %bitcast.12, s32[1,64]{1,0:T(1,128)} %bitcast.13, ...), custom_call_target="tpu_custom_call" | custom-call | tf_op jit(solution)/shard_map/pallas_call | solution.py:407
  35.6 0.0 copy-start
  35.6 1.6 %copy.13 = f32[32,1024]{1,0:T(8,128)} copy(f32[32,1024]{1,0:T(8,128)} %get-tuple-element.8) | data formatting | bytes 262144
  37.2 0.0 copy-done
  37.2 0.7 %copy.14 = f32[64,4,128]{2,1,0:T(4,128)} copy(f32[64,4,128]{2,1,0:T(4,128)S(1)} %bitcast.8) | data formatting | bytes 262144
Async XLA Ops:
  35.6 1.6 %copy-start = (f32[256,128]{1,0:T(8,128)S(1)}, f32[256,128]{1,0:T(8,128)}, u32[]{:S(2)}) copy-start(f32[256,128]{1,0:T(8,128)} %get-tuple-element.5) | copy-start | bytes 393220

commit v5 on v4

--- a/solution.py
+++ b/solution.py
@@ -73,8 +73,8 @@
 ORDERS = (("x", "y", "z"), ("y", "z", "x"), ("z", "x", "y"))
 
 
-def kernel(sizes, st, stations, times, partner, wave_in, station_in, time_in, tiles_in, fwd_in, inv_in, ends_in, stack, diff,
-           data, near_data, wave, tiles, fwd, inv, ends, rows, station_row, time_row, mine, words, packed,
+def kernel(sizes, st_in, stations_in, times_in, partner_in, wave_in, station_in, time_in, tiles_in, fwd_in, inv_in, ends_in, stack, diff,
+           data, near_data, wave, tiles, fwd, inv, ends, rows, station_row, time_row, mine, words, packed, st, stations, times, partner,
            xr, xi, wb, rw, pb, sb, xf, pw, lw, lr, li, lq, pq, er, ei, gr, gi,
            send_sem, recv_sem, near_sem, word_sem, load_sem):
     ngx, ngy = sizes
@@ -97,7 +97,7 @@
     loads = []
     for i, (source, target) in enumerate(
         ((wave_in, wave), (station_in, station_row), (time_in, time_row), (fwd_in, fwd), (tiles_in, tiles),
-         (inv_in, inv), (ends_in, ends))
+         (inv_in, inv), (ends_in, ends), (st_in, st), (stations_in, stations), (times_in, times), (partner_in, partner))
     ):
         copy = pltpu.make_async_copy(source, target, load_sem.at[i])
         copy.start()
@@ -110,11 +110,22 @@
         (gx, (gy + ngy - 1) % ngy),
     )
     sibling = device(moved("core", 1))
-    peers = [device(moved(axis, r)) for axis in ("x", "y", "z") for r in range(1, dims[axis])]
-    peers = peers + [sibling] + list(near)
+    side = dims["z"]
+
+    def across(c, n):
+        first, second = ORDERS[c][:2]
+        return {**here, first: (here[first] + n % side) % side, second: (here[second] + n // side) % side}
+
     barrier = pltpu.get_barrier_semaphore()
-    for peer in peers:
+    for peer in (sibling,) + near:
         pl.semaphore_signal(barrier, inc=1, device_id=peer, device_id_type=mesh_id)
+
+    def greet(n, carry):
+        for c in range(3):
+            pl.semaphore_signal(barrier, inc=1, device_id=device(across(c, n)), device_id_type=mesh_id)
+        return carry
+
+    lax.fori_loop(1, side * side, greet, 0)
 
     loads[0].wait()
     for c in range(3):
@@ -126,7 +137,7 @@
     loads[2].wait()
     mine[...] = jnp.zeros_like(mine)
     mine[:, 0:DET] = station_row[...] * 2048 + time_row[...]
-    pl.semaphore_wait(barrier, len(peers))
+    pl.semaphore_wait(barrier, 5 + 3 * (side * side - 1))
 
     def send(source, target, to, send_at, recv_at):
         return pltpu.make_async_remote_copy(
@@ -139,32 +150,34 @@
         ref = data.at[place(coords, whole) + (c,)]
         return send(ref, ref, to, send_sem.at[c, index], recv_sem.at[c, index])
 
-    def phase_copy(c, phase, r):
-        order = ORDERS[c]
-        return block_copy(here, order[:phase], c, device(moved(order[phase], r)), 3 * phase + r - 1)
-
-    def steps(c, phase):
-        count = dims[ORDERS[c][phase]]
-        return [r for r in (1, 3, 2) if r < count]
-
-    def start_phase(phase):
-        for c in range(3):
-            if phase:
-                for r in steps(c, phase - 1):
-                    phase_copy(c, phase - 1, r).wait_recv()
-            for r in steps(c, phase):
-                phase_copy(c, phase, r).start()
+    def own_copy(c, n):
+        return block_copy(here, (), c, device(across(c, n)), n - 1)
+
+    def line_copy(c, r):
+        return block_copy(here, ORDERS[c][:2], c, device(moved(ORDERS[c][2], r)), 14 + r)
+
+    def each_own(act):
+        def step(n, carry):
+            for c in range(3):
+                act(own_copy(c, n))
+            return carry
+
+        lax.fori_loop(1, side * side, step, 0)
+
+    steps = [r for r in (1, 3, 2) if r < side]
 
     def plane_copy(c, r):
-        return block_copy(moved(ORDERS[c][2], -r), ORDERS[c][:2], c, sibling, 9 + r)
-
-    start_phase(0)
+        return block_copy(moved(ORDERS[c][2], -r), ORDERS[c][:2], c, sibling, 18 + r)
+
     own_block = data.at[place(here, ()) + (slice(None),)]
     near_copies = []
     for d in range(4):
         near_copies.append(send(mine, words.at[d ^ 1], near[d], word_sem.at[0, d], word_sem.at[1, d ^ 1]))
         near_copies.append(send(own_block, near_data.at[d ^ 1], near[d], near_sem.at[0, d], near_sem.at[1, d ^ 1]))
-    for copy in near_copies:
+    for copy in near_copies[::2]:
+        copy.start()
+    each_own(lambda copy: copy.start())
+    for copy in near_copies[1::2]:
         copy.start()
 
     for copy in loads[3:]:
@@ -182,7 +195,12 @@
         wb[2 * b] = real * scale
         wb[2 * b + 1] = imag * scale
 
-    start_phase(1)
+    each_own(lambda copy: copy.wait_recv())
+    for r in steps:
+        for c in range(3):
+            line_copy(c, r).start()
+    for c in range(3):
+        plane_copy(c, 0).start()
 
     moves = ((1, 0), (-1, 0), (0, 1), (0, -1))
     span = 2 * SB
@@ -191,7 +209,7 @@
     valid = []
     for copy in near_copies:
         copy.wait_recv()
-    to_scalars = pltpu.make_async_copy(words, packed, load_sem.at[7])
+    to_scalars = pltpu.make_async_copy(words, packed, load_sem.at[11])
     to_scalars.start()
     for d, (dx, dy) in enumerate(moves + ((0, 0),)):
         nx, ny = gx + dx, gy + dy
@@ -231,10 +249,6 @@
 
     lax.fori_loop(0, DET, cut_step, 0, unroll=4)
 
-    start_phase(2)
-    for c in range(3):
-        plane_copy(c, 0).start()
-
     lr[...], li[...] = transform(lw[...].astype(BF16), forward)
     for d in range(4):
         er[d], ei[d] = transform(pw[d].astype(BF16), forward)
@@ -265,7 +279,7 @@
     for d in range(4):
         raw = inverse_dot(gathered(gr, d), gathered(gi, d), inv[...])
         scale = local_scale * lax.rsqrt(mean_of(pq, d) + EPS) * valid[d]
-        diff[pl.ds(d, DET, stride=4), :] = raw * scale
+        diff[:, d, :] = raw * scale
 
     def transform_plane(c, coords):
         order = ORDERS[c]
@@ -303,8 +317,6 @@
 
         lax.fori_loop(0, dims["y"], step, 0)
 
-    side = dims["z"]
-
     def turn(o):
         return o + (o // 2) * (1 - 2 * (o % 2))
 
@@ -313,7 +325,7 @@
         for c in range(3):
             @pl.when(o > 0)
             def _():
-                block_copy(here, ORDERS[c][:2], c, device(moved(ORDERS[c][2], r)), 5 + r).wait_recv()
+                line_copy(c, r).wait_recv()
                 plane_copy(c, r).start()
         for c in range(3):
             transform_plane(c, moved(ORDERS[c][2], -r))
@@ -376,10 +388,10 @@
 
     for copy in near_copies:
         copy.wait_send()
+    each_own(lambda copy: copy.wait_send())
     for c in range(3):
-        for phase in range(3):
-            for r in steps(c, phase):
-                phase_copy(c, phase, r).wait_send()
+        for r in steps:
+            line_copy(c, r).wait_send()
         for r in range(side):
             plane_copy(c, r).wait_send()
 
@@ -389,11 +401,10 @@
     groups = ngx * ngy
     count = templates.shape[0] * templates.shape[1]
     forward, inverse, ends = tables()
-    smem = pl.BlockSpec(memory_space=pltpu.SMEM)
     vmem = pl.BlockSpec(memory_space=pltpu.VMEM)
-    anywhere = pl.BlockSpec(memory_space=pl.ANY)
+    hbm = pl.BlockSpec(memory_space=pltpu.HBM)
     dims = ring_layout(ngx, ngy)
-    ntpl = templates.shape[0]
+    ntpl, slots = templates.shape[:2]
 
     def floats(*shape):
         return pltpu.VMEM(shape, F32)
@@ -408,9 +419,9 @@
         functools.partial(kernel, (ngx, ngy)),
         out_shape=(
             jax.ShapeDtypeStruct((ntpl, LB * B), F32),
-            jax.ShapeDtypeStruct((4 * DET, B), F32),
+            jax.ShapeDtypeStruct((DET, 4, B), F32),
         ),
-        in_specs=[smem] * 4 + [anywhere] * 7,
+        in_specs=[hbm] * 11,
         out_specs=(vmem, vmem),
         scratch_shapes=[
             halves(dims["y"], dims["x"], dims["z"], 2, 3, 2 * SB, B),
@@ -426,6 +437,10 @@
             ints(1, B),
             ints(4, 1, B),
             pltpu.SMEM((4, 1, B), jnp.int32),
+            pltpu.SMEM((slots, ntpl), jnp.int32),
+            pltpu.SMEM((DET,), jnp.int32),
+            pltpu.SMEM((DET,), jnp.int32),
+            pltpu.SMEM((4, DET), jnp.int32),
             floats(groups * 6, 16, B),
             floats(groups * 6, 16, B),
             floats(6 * TB, count, B),
@@ -443,19 +458,19 @@
             floats(4, 12 * DET, B),
             floats(4, 8 * DET, B),
             floats(4, 8 * DET, B),
-            pltpu.SemaphoreType.DMA((3, 13)),
-            pltpu.SemaphoreType.DMA((3, 13)),
+            pltpu.SemaphoreType.DMA((3, 22)),
+            pltpu.SemaphoreType.DMA((3, 22)),
             pltpu.SemaphoreType.DMA((2, 4)),
             pltpu.SemaphoreType.DMA((2, 4)),
-            pltpu.SemaphoreType.DMA((8,)),
+            pltpu.SemaphoreType.DMA((12,)),
         ],
         compiler_params=pltpu.CompilerParams(
-            collective_id=0, has_side_effects=True, vmem_limit_bytes=60 * 1024 * 1024
+            collective_id=0, has_side_effects=True, vmem_limit_bytes=59 * 1024 * 1024
         ),
     )(tpl_stations.T, det_station, det_time, partner.T, jnp.transpose(waveforms, (1, 0, 2)),
       det_station.reshape(1, DET), det_time.reshape(1, DET), templates.reshape(count, 3 * TB * B),
       jnp.asarray(forward), jnp.asarray(inverse), jnp.asarray(ends))
-    return stack, diff.reshape(DET, 4, B)
+    return stack, diff
 
 
 def solution(mesh):

time: 38.1 us -> 36.8 us (0.966)
  Pallas kernels: 35 us -> 33.7 us
    pallas_call x1, Pallas kernels: 35 us -> 33.7 us  [on_device(): pl.pallas_call(functools.partial(kernel, (ngx, ngy)), out_shape=(jax.Shap...]
where the time goes in v5:
time: 36.8 us; the launch traced here: 36.6 us
  Pallas kernels  33.7 us (92%)
  local copies, waits for them, and re-layouts  2.26 us (6%)
  between operations  0.65 us (2%)
    pallas_call x1, Pallas kernels, on_device(): pl.pallas_call(functools.partial(kernel, (ngx, ngy)), out_shape=(jax.Shap...  33.7 us
    unnamed x4, local copies, waits for them, and re-layouts  2.26 us

profile of v5, /device:TPU:1, one launch (start us, length us, event | category | flops | bytes accessed | tf_op | source)
XLA Modules:
  0.0 36.6 jit_solution(8367317663590555473)
XLA Ops:
  0.6 33.7 %shard_map.104 = (f32[32,1024]{1,0:T(8,128)}, f32[64,4,128]{2,1,0:T(4,128)}) custom-call(s32[8,32]{1,0:T(8,128)} %bitcast.8, s32[64]{0:T(128)} %stations_in.1, s32[64]{0:T(128)} %times_in.1, s32[4,64]{1,0:T(4,128)} %bitcast.9, bf16[3,2,1536]{2,1,0:T(2,128)(2,1)} %bitcast.7, s32[1,64]{1,0:T(1,128)} %bitcast.10, s32[1,64]{1,0:T(1,128)} %bitcast.11, ...), custom_call_target="tpu_custom_call" | custom-call | tf_op jit(solution)/shard_map/pallas_call | solution.py:418
  34.3 0.0 copy-start
  34.4 1.6 %copy.13 = f32[32,1024]{1,0:T(8,128)} copy(f32[32,1024]{1,0:T(8,128)} %get-tuple-element.4) | data formatting | bytes 262144
  36.0 0.0 copy-done
  36.0 0.7 %copy.14 = f32[64,4,128]{2,1,0:T(4,128)} copy(f32[64,4,128]{2,1,0:T(4,128)S(1)} %copy-done) | data formatting | bytes 262144
Async XLA Ops:
  34.3 1.6 %copy-start = (f32[64,4,128]{2,1,0:T(4,128)S(1)}, f32[64,4,128]{2,1,0:T(4,128)}, u32[]{:S(2)}) copy-start(f32[64,4,128]{2,1,0:T(4,128)} %get-tuple-element.5) | copy-start | bytes 393220

commit v6 on v5

--- a/solution.py
+++ b/solution.py
@@ -247,7 +247,7 @@
             pq[d, at, :] = first * first * mask_first + second * second * mask_last
         return carry
 
-    lax.fori_loop(0, DET, cut_step, 0, unroll=4)
+    lax.fori_loop(0, DET, cut_step, 0, unroll=8)
 
     lr[...], li[...] = transform(lw[...].astype(BF16), forward)
     for d in range(4):
@@ -367,7 +367,7 @@
         return carry
 
     lax.fori_loop(0, templates, product_step, 0)
-    group = 2
+    group = 4
 
     def back_step(i, carry):
         size = group * slots * LB

time: 36.8 us -> 35.9 us (0.976)
  Pallas kernels: 33.7 us -> 32.8 us
    pallas_call x1, Pallas kernels: 33.7 us -> 32.8 us  [on_device(): pl.pallas_call(functools.partial(kernel, (ngx, ngy)), out_shape=(jax.Shap...]
where the time goes in v6:
time: 35.9 us; the launch traced here: 35.7 us
  Pallas kernels  32.8 us (91%)
  local copies, waits for them, and re-layouts  2.26 us (6%)
  between operations  0.65 us (2%)
    pallas_call x1, Pallas kernels, on_device(): pl.pallas_call(functools.partial(kernel, (ngx, ngy)), out_shape=(jax.Shap...  32.8 us
    unnamed x4, local copies, waits for them, and re-layouts  2.26 us

profile of v6, /device:TPU:1, one launch (start us, length us, event | category | flops | bytes accessed | tf_op | source)
XLA Modules:
  0.0 35.7 jit_solution(17005090509979940566)
XLA Ops:
  0.6 32.8 %shard_map.104 = (f32[32,1024]{1,0:T(8,128)}, f32[64,4,128]{2,1,0:T(4,128)}) custom-call(s32[8,32]{1,0:T(8,128)} %bitcast.8, s32[64]{0:T(128)} %stations_in.1, s32[64]{0:T(128)} %times_in.1, s32[4,64]{1,0:T(4,128)} %bitcast.9, bf16[3,2,1536]{2,1,0:T(2,128)(2,1)} %bitcast.7, s32[1,64]{1,0:T(1,128)} %bitcast.10, s32[1,64]{1,0:T(1,128)} %bitcast.11, ...), custom_call_target="tpu_custom_call" | custom-call | tf_op jit(solution)/shard_map/pallas_call | solution.py:418
  33.5 0.0 copy-start
  33.5 1.6 %copy.13 = f32[32,1024]{1,0:T(8,128)} copy(f32[32,1024]{1,0:T(8,128)} %get-tuple-element.4) | data formatting | bytes 262144
  35.1 0.0 copy-done
  35.1 0.7 %copy.14 = f32[64,4,128]{2,1,0:T(4,128)} copy(f32[64,4,128]{2,1,0:T(4,128)S(1)} %copy-done) | data formatting | bytes 262144
Async XLA Ops:
  33.5 1.6 %copy-start = (f32[64,4,128]{2,1,0:T(4,128)S(1)}, f32[64,4,128]{2,1,0:T(4,128)}, u32[]{:S(2)}) copy-start(f32[64,4,128]{2,1,0:T(4,128)} %get-tuple-element.5) | copy-start | bytes 393220

commit v7 on v6

--- a/solution.py
+++ b/solution.py
@@ -315,7 +315,7 @@
                     rw[2 * linear(full) + sta] = out[begin : begin + LB]
             return carry
 
-        lax.fori_loop(0, dims["y"], step, 0)
+        lax.fori_loop(0, dims["y"], step, 0, unroll=2)
 
     def turn(o):
         return o + (o // 2) * (1 - 2 * (o % 2))

time: 35.9 us -> 35.5 us (0.989)
  no operation moved by 1% of the time
where the time goes in v7:
time: 35.5 us; the launch traced here: 35.4 us
  Pallas kernels  32.5 us (92%)
  local copies, waits for them, and re-layouts  2.26 us (6%)
  between operations  0.65 us (2%)
    pallas_call x1, Pallas kernels, on_device(): pl.pallas_call(functools.partial(kernel, (ngx, ngy)), out_shape=(jax.Shap...  32.5 us
    unnamed x4, local copies, waits for them, and re-layouts  2.26 us

profile of v7, /device:TPU:1, one launch (start us, length us, event | category | flops | bytes accessed | tf_op | source)
XLA Modules:
  0.0 35.4 jit_solution(13341764255242439406)
XLA Ops:
  0.6 32.5 %shard_map.104 = (f32[32,1024]{1,0:T(8,128)}, f32[64,4,128]{2,1,0:T(4,128)}) custom-call(s32[8,32]{1,0:T(8,128)} %bitcast.8, s32[64]{0:T(128)} %stations_in.1, s32[64]{0:T(128)} %times_in.1, s32[4,64]{1,0:T(4,128)} %bitcast.9, bf16[3,2,1536]{2,1,0:T(2,128)(2,1)} %bitcast.7, s32[1,64]{1,0:T(1,128)} %bitcast.10, s32[1,64]{1,0:T(1,128)} %bitcast.11, ...), custom_call_target="tpu_custom_call" | custom-call | tf_op jit(solution)/shard_map/pallas_call | solution.py:418
  33.1 0.0 copy-start
  33.2 1.6 %copy.13 = f32[32,1024]{1,0:T(8,128)} copy(f32[32,1024]{1,0:T(8,128)} %get-tuple-element.4) | data formatting | bytes 262144
  34.8 0.0 copy-done
  34.8 0.7 %copy.14 = f32[64,4,128]{2,1,0:T(4,128)} copy(f32[64,4,128]{2,1,0:T(4,128)S(1)} %copy-done) | data formatting | bytes 262144
Async XLA Ops:
  33.1 1.6 %copy-start = (f32[64,4,128]{2,1,0:T(4,128)S(1)}, f32[64,4,128]{2,1,0:T(4,128)}, u32[]{:S(2)}) copy-start(f32[64,4,128]{2,1,0:T(4,128)} %get-tuple-element.5) | copy-start | bytes 393220
